TPU v7x, 256 devices: a whole 4x4x8 slice. The times are simulated.
256 devices in a mesh: clip: 4 (over z_lo), seg: 64 (over x, y, z_hi, core).
Axes of the slice: x: 4, y: 4, z: 8 (z_hi: 2, z_lo: 4; z = z_hi * 4 + z_lo), core: 2. Of those that a mesh axis runs over, the one named last changes fastest.
Arguments:
- spectra: bfloat16 [16, 2, 1024, 1536], P('clip', None, 'seg'), may hold values from -6 to 6
- target: bfloat16 [16, 786432], P('clip', 'seg'), may hold values from -12 to 12
- lengths: int32 [16], P('clip'), may hold values from 768 to 1536, as said below
Outputs:
- loss: float32 [], replicated
- spec_grad: bfloat16 [16, 2, 1024, 1536], P('clip', None, 'seg')
Inputs may be any that keep to these rules, and one draw needn't show every extreme that they name: `lengths`: some clip has all 1536 frames.
All inputs are finite; a program needn't handle non-finite values.
Results may differ from a plain program's by a relative error of at most 0.0092.
Values may be sent and summed in bfloat16 or wider, within the bound.
A program may use at most 128 MiB of HBM per device.

v0:
```python
from functools import partial
import math

import jax
import jax.numpy as jnp
from jax import lax
from jax.sharding import Mesh
from jax.sharding import PartitionSpec as P

BINS = 1024
NFFT = 2048
HOP = 512
SEG = ("seg_0", "seg_1", "seg_2", "seg_3")


EPS_MAG = 0.1
EPS_RATIO = 1e-05


def shifted(block, axis, distance):
    devices = range(lax.axis_size(axis))
    route = [(i - distance, i) for i in devices if i - distance in devices]
    return lax.ppermute(block, axis, route)


def over_axes(x, axes):
    for axis in axes:
        x = lax.psum(x, axis)
    return x


def from_everyone(x, axis):
    devices = lax.axis_size(axis)
    return lax.all_to_all(jnp.broadcast_to(x[None], (devices, *x.shape)), axis, 0, 0, tiled=True)


def of_everyone(x, axis):
    return from_everyone(x, axis).sum(axis=0)


def wave_table(bins_index, time_index, points, factor):
    halfway = points // 2
    is_sine = bins_index >= halfway
    harmonic = jnp.where(is_sine, bins_index - halfway, bins_index)
    angles = (harmonic * time_index % points).astype(jnp.float32) * (2.0 * math.pi / points)
    window = 0.5 - 0.5 * jnp.cos(time_index.astype(jnp.float32) * (2.0 * math.pi / points))
    entry_value = jnp.where(is_sine, -jnp.sin(angles), jnp.cos(angles))
    return (entry_value * window * factor).astype(jnp.bfloat16)


def analysis_rows(points, anchor, height):
    time_index = anchor + jnp.arange(height, dtype=jnp.int32)
    return wave_table(
        jnp.arange(points, dtype=jnp.int32)[None, :],
        time_index[:, None],
        points,
        1.0 / math.sqrt(points),
    )


def analysis_cols(points, anchor, height):
    bins_index = anchor + jnp.arange(height, dtype=jnp.int32)
    return wave_table(
        bins_index[:, None],
        jnp.arange(points, dtype=jnp.int32)[None, :],
        points,
        1.0 / math.sqrt(points),
    )


def synth_rows(anchor, height):
    bins_index = anchor + jnp.arange(height, dtype=jnp.int32)
    return wave_table(
        bins_index[:, None], jnp.arange(NFFT, dtype=jnp.int32)[None, :], NFFT, 1.0 / math.sqrt(BINS)
    )


def synth_cols(anchor, height):
    time_index = anchor + jnp.arange(height, dtype=jnp.int32)
    return wave_table(
        jnp.arange(2 * BINS, dtype=jnp.int32)[None, :],
        time_index[:, None],
        NFFT,
        1.0 / math.sqrt(BINS),
    )


def blocked_product(operand, along, make_rows, pattern, out_shape):
    length_in = operand.shape[along]
    stride = min(512, length_in)

    def turn(turn_index, summed):
        anchor = turn_index * stride
        portion = lax.dynamic_slice_in_dim(operand, anchor, stride, along)
        return summed + jnp.einsum(
            pattern, portion, make_rows(anchor, stride), preferred_element_type=jnp.float32
        )

    return lax.fori_loop(0, length_in // stride, turn, jnp.zeros(out_shape, jnp.float32))


def spread_parts(quarters):
    return sum(
        (
            jnp.pad(quarters[:, :, quarter], ((0, 0), (quarter, 3 - quarter), (0, 0)))
            for quarter in range(4)
        )
    )


def framed(signal, beyond, stride):
    frame_count = signal.shape[1] // stride
    padded = jnp.concatenate([signal, beyond], axis=1).reshape(
        signal.shape[0], frame_count + 3, stride
    )
    return jnp.concatenate(
        [padded[:, quarter : quarter + frame_count] for quarter in range(4)], axis=2
    )


def body(spectra, target, lengths):
    clip_count = spectra.shape[0]
    frames_all = spectra.shape[3]
    samples = target.shape[1]
    rows_here = samples // HOP
    seg_index = lax.axis_index(SEG)
    start_sample = seg_index * samples
    block = lax.all_to_all(spectra, SEG, split_axis=3, concat_axis=2, tiled=True)
    stacked = block.reshape(block.shape[0], 2 * BINS, block.shape[3])
    signals = blocked_product(
        stacked, 1, synth_rows, "ckf,km->cfm", (block.shape[0], block.shape[3], NFFT)
    )
    spilled = spread_parts(signals.reshape(clip_count, rows_here, 4, HOP))
    spill = shifted(spilled[:, rows_here:], SEG, 1)
    estimate = (
        spilled[:, :rows_here] + jnp.pad(spill, ((0, 0), (0, rows_here - 3), (0, 0)))
    ).reshape(clip_count, samples)
    sample_index = start_sample + jnp.arange(samples, dtype=jnp.int32)
    inside = sample_index[None, :] < (lengths * HOP)[:, None]
    est_wave = jnp.where(inside, estimate, 0.0).astype(jnp.bfloat16)
    clean = jnp.where(inside, target, jnp.zeros_like(target))
    sizes_list = (NFFT // 4, NFFT // 2, NFFT)
    beyond_est, beyond_tgt = shifted((est_wave[:, : 3 * HOP], clean[:, : 3 * HOP]), SEG, -1)
    beyond_list = [
        (beyond_est[:, : 3 * (points // 4)], beyond_tgt[:, : 3 * (points // 4)])
        for points in sizes_list
    ]
    saved = []
    spread_list = []
    energy_list = []
    logterm_list = []
    for points, beyond_pair in zip(sizes_list, beyond_list):
        stride = points // 4
        halfway = points // 2
        frame_count = samples // stride
        paired = jnp.stack(
            [framed(est_wave, beyond_pair[0], stride), framed(clean, beyond_pair[1], stride)]
        )
        spectra_pair = blocked_product(
            paired,
            3,
            partial(analysis_rows, points),
            "ecfm,mj->ecfj",
            (2, clip_count, frame_count, points),
        )
        est_real = spectra_pair[0, :, :, :halfway]
        est_imag = spectra_pair[0, :, :, halfway:]
        tgt_real = spectra_pair[1, :, :, :halfway]
        tgt_imag = spectra_pair[1, :, :, halfway:]
        est_mag = jnp.sqrt(est_real * est_real + est_imag * est_imag + EPS_MAG)
        tgt_mag = jnp.sqrt(tgt_real * tgt_real + tgt_imag * tgt_imag + EPS_MAG)
        usable_count = lengths * (HOP // stride)
        frame_index = start_sample // stride + jnp.arange(frame_count, dtype=jnp.int32)
        usable = frame_index[None, :, None] < usable_count[:, None, None]
        mag_gap = est_mag - tgt_mag
        log_gap = jnp.log(est_mag) - jnp.log(tgt_mag)
        entries = (usable_count * halfway).astype(jnp.float32)
        spread_list.append(jnp.sum(jnp.where(usable, mag_gap * mag_gap, 0.0), axis=(1, 2)))
        energy_list.append(jnp.sum(jnp.where(usable, tgt_mag * tgt_mag, 0.0), axis=(1, 2)))
        logterm_list.append(
            jnp.sum(jnp.where(usable, log_gap * log_gap, 0.0), axis=(1, 2)) / entries
        )
        saved.append((est_real, est_imag, est_mag, mag_gap, log_gap, usable, entries))
    spreads = jnp.stack(spread_list)
    energies = jnp.stack(energy_list)
    logterms = jnp.stack(logterm_list)
    spreads, energies, logterms = (
        over_axes(spreads, SEG),
        over_axes(energies, SEG),
        over_axes(logterms, SEG),
    )
    own_loss = jnp.sum(jnp.sqrt((spreads + EPS_RATIO) / energies) + logterms)
    loss = of_everyone(own_loss, "clip") / (3 * clip_count * lax.axis_size("clip"))
    ratio_weight = 1.0 / jnp.sqrt((spreads + EPS_RATIO) * energies)
    gradient = jnp.zeros((clip_count, samples), jnp.float32)
    extras = []
    for level, points in enumerate(sizes_list):
        stride = points // 4
        frame_count = samples // stride
        est_real, est_imag, est_mag, mag_gap, log_gap, usable, entries = saved[level]
        grad_mag = jnp.where(
            usable,
            mag_gap * ratio_weight[level][:, None, None]
            + 2.0 * log_gap / (est_mag * entries[:, None, None]),
            0.0,
        ) * (frames_all * BINS)
        grad_x = jnp.concatenate(
            [grad_mag * est_real / est_mag, grad_mag * est_imag / est_mag], axis=2
        ).astype(jnp.bfloat16)
        grad_frames = blocked_product(
            grad_x,
            2,
            partial(analysis_cols, points),
            "cfj,jm->cfm",
            (clip_count, frame_count, points),
        )
        spread_back = spread_parts(grad_frames.reshape(clip_count, frame_count, 4, stride))
        gradient = gradient + spread_back[:, :frame_count].reshape(clip_count, samples)
        extras.append(spread_back[:, frame_count:].reshape(clip_count, 3 * stride))
    joined = sum(
        (jnp.pad(portion, ((0, 0), (0, 3 * HOP - portion.shape[1]))) for portion in extras)
    )
    received = shifted(joined, SEG, 1)
    gradient = gradient + jnp.pad(received, ((0, 0), (0, samples - 3 * HOP)))
    grad_wave = jnp.where(inside, gradient, 0.0).astype(jnp.bfloat16)
    grad_hops = grad_wave.reshape(clip_count, rows_here, HOP)
    following = shifted(grad_hops[:, :3], SEG, -1)
    extended = jnp.concatenate([grad_hops, following], axis=1)
    grad_signals = jnp.concatenate(
        [extended[:, quarter : quarter + rows_here] for quarter in range(4)], axis=2
    )
    grad_time = blocked_product(
        grad_signals, 2, synth_cols, "cfm,mk->ckf", (clip_count, 2 * BINS, rows_here)
    )
    rounded = grad_time.reshape(clip_count, 2, BINS, rows_here).astype(jnp.bfloat16)
    spec_grad = lax.all_to_all(rounded, SEG, split_axis=2, concat_axis=3, tiled=True)
    return (loss, spec_grad)


def solution(mesh):
    finer = Mesh(
        mesh.devices.reshape(mesh.shape["clip"], 4, 4, 2, 2),
        ("clip", "seg_0", "seg_1", "seg_2", "seg_3"),
    )
    placed = (P("clip", None, SEG, None), P("clip", SEG), P("clip"))
    return jax.shard_map(
        body,
        mesh=finer,
        in_specs=placed,
        out_specs=(P(), P("clip", None, SEG, None)),
        check_vma=False,
    )
```

profile of v0, /device:TPU:33, one launch (start us, length us, event | category | flops | bytes accessed | tf_op | source)
XLA Modules:
  0.0 549.3 jit_solution(1532712928770241731)
XLA Ops:
  54.4 70.7 %while.106 = (s32[]{:T(128)}, f32[4,24,2048]{2,1,0:T(8,128)S(1)}, bf16[4,2048,24]{1,2,0:T(8,128)(2,1)S(1)}, s32[]{:T(128)}, s32[]{:T(128)}, /*index=5*/s32[]{:T(128)}, s32[]{:T(128)}) while((s32[]{:T(128)}, f32[4,24,2048]{2,1,0:T(8,128)S(1)}, bf16[4,2048,24]{1,2,0:T(8,128)(2,1)S(1)}, s32[]{:T(128)}, s32[]{:T(128)}, ...), condition=%wide.region_1.2_spmd.clone, body=%wide.region_0.1_spmd.clone.sunk | while | flops 221654016 | bytes 1692817 | solution.py:99
  54.7 17.4 %convolution_add_fusion.8 = f32[4,24,2048]{2,1,0:T(8,128)S(1)} fusion(f32[2048]{0:T(1024)S(1)} %multiply_subtract_fusion.13, s32[512]{0:T(512)S(1)} %add_select_fusion.21, pred[512]{0:T(512)(128)(4,1)S(1)} %fusion.240, f32[4,24,2048]{2,1,0:T(8,128)S(1)} %get-tuple-element.896, pred[]{:T(512)S(6)} %compare.52, ...), kind=kOutput, calls=%fused_computation.10.clone.1 | convolution fusion | flops 221642752 | bytes 1681925 | tf_op jit(solution)/shard_map/while/body/eval_jaxpr/ckf,km->cfm/dot_general | solution.py:95
  72.2 17.4 %convolution_add_fusion.8 = f32[4,24,2048]{2,1,0:T(8,128)S(1)} fusion(f32[2048]{0:T(1024)S(1)} %multiply_subtract_fusion.13, s32[512]{0:T(512)S(1)} %add_select_fusion.21, pred[512]{0:T(512)(128)(4,1)S(1)} %fusion.240, f32[4,24,2048]{2,1,0:T(8,128)S(1)} %get-tuple-element.896, pred[]{:T(512)S(6)} %compare.52, ...), kind=kOutput, calls=%fused_computation.10.clone.1 | convolution fusion | flops 221642752 | bytes 1681925 | tf_op jit(solution)/shard_map/while/body/eval_jaxpr/ckf,km->cfm/dot_general | solution.py:95
  89.8 17.4 %convolution_add_fusion.8 = f32[4,24,2048]{2,1,0:T(8,128)S(1)} fusion(f32[2048]{0:T(1024)S(1)} %multiply_subtract_fusion.13, s32[512]{0:T(512)S(1)} %add_select_fusion.21, pred[512]{0:T(512)(128)(4,1)S(1)} %fusion.240, f32[4,24,2048]{2,1,0:T(8,128)S(1)} %get-tuple-element.896, pred[]{:T(512)S(6)} %compare.52, ...), kind=kOutput, calls=%fused_computation.10.clone.1 | convolution fusion | flops 221642752 | bytes 1681925 | tf_op jit(solution)/shard_map/while/body/eval_jaxpr/ckf,km->cfm/dot_general | solution.py:95
  107.3 17.4 %convolution_add_fusion.8 = f32[4,24,2048]{2,1,0:T(8,128)S(1)} fusion(f32[2048]{0:T(1024)S(1)} %multiply_subtract_fusion.13, s32[512]{0:T(512)S(1)} %add_select_fusion.21, pred[512]{0:T(512)(128)(4,1)S(1)} %fusion.240, f32[4,24,2048]{2,1,0:T(8,128)S(1)} %get-tuple-element.896, pred[]{:T(512)S(6)} %compare.52, ...), kind=kOutput, calls=%fused_computation.10.clone.1 | convolution fusion | flops 221642752 | bytes 1681925 | tf_op jit(solution)/shard_map/while/body/eval_jaxpr/ckf,km->cfm/dot_general | solution.py:95
  145.8 74.5 %while.108 = (s32[]{:T(128)}, f32[2,4,24,2048]{3,2,1,0:T(8,128)S(1)}, bf16[2,4,24,2048]{3,2,1,0:T(8,128)(2,1)}, s32[]{:T(128)}, s32[]{:T(128)}, /*index=5*/s32[]{:T(128)}, s32[]{:T(128)}) while((s32[]{:T(128)}, f32[2,4,24,2048]{3,2,1,0:T(8,128)S(1)}, bf16[2,4,24,2048]{3,2,1,0:T(8,128)(2,1)}, s32[]{:T(128)}, s32[]{:T(128)}, ...), condition=%wide.region_7.8_spmd.clone, body=%wide.region_6.7_spmd.clone.sunk | while | flops 423373824 | bytes 3371153 | solution.py:99
  146.1 18.4 %convolution_add_fusion.9 = f32[2,4,24,2048]{3,2,1,0:T(8,128)S(1)} fusion(f32[512]{0:T(512)S(1)} %multiply_subtract_fusion.15, s32[512]{0:T(512)S(1)} %iota_add_fusion.14, s32[2048]{0:T(1024)S(1)} %add_select_fusion.23, pred[2048]{0:T(1024)(128)(4,1)S(1)} %iota_compare_fusion.8, f32[2,4,24,2048]{3,2,1,0:T(8,128)S(1)} %get-tuple-element.938, ...), kind=kOutput, calls=%fused_computation.69.clone.1 | convolution fusion | flops 423362560 | bytes 3356677 | tf_op jit(solution)/shard_map/while/body/eval_jaxpr/ecfm,mj->ecfj/dot_general | solution.py:95
  164.6 18.4 %convolution_add_fusion.9 = f32[2,4,24,2048]{3,2,1,0:T(8,128)S(1)} fusion(f32[512]{0:T(512)S(1)} %multiply_subtract_fusion.15, s32[512]{0:T(512)S(1)} %iota_add_fusion.14, s32[2048]{0:T(1024)S(1)} %add_select_fusion.23, pred[2048]{0:T(1024)(128)(4,1)S(1)} %iota_compare_fusion.8, f32[2,4,24,2048]{3,2,1,0:T(8,128)S(1)} %get-tuple-element.938, ...), kind=kOutput, calls=%fused_computation.69.clone.1 | convolution fusion | flops 423362560 | bytes 3356677 | tf_op jit(solution)/shard_map/while/body/eval_jaxpr/ecfm,mj->ecfj/dot_general | solution.py:95
  183.1 18.4 %convolution_add_fusion.9 = f32[2,4,24,2048]{3,2,1,0:T(8,128)S(1)} fusion(f32[512]{0:T(512)S(1)} %multiply_subtract_fusion.15, s32[512]{0:T(512)S(1)} %iota_add_fusion.14, s32[2048]{0:T(1024)S(1)} %add_select_fusion.23, pred[2048]{0:T(1024)(128)(4,1)S(1)} %iota_compare_fusion.8, f32[2,4,24,2048]{3,2,1,0:T(8,128)S(1)} %get-tuple-element.938, ...), kind=kOutput, calls=%fused_computation.69.clone.1 | convolution fusion | flops 423362560 | bytes 3356677 | tf_op jit(solution)/shard_map/while/body/eval_jaxpr/ecfm,mj->ecfj/dot_general | solution.py:95
  201.6 18.4 %convolution_add_fusion.9 = f32[2,4,24,2048]{3,2,1,0:T(8,128)S(1)} fusion(f32[512]{0:T(512)S(1)} %multiply_subtract_fusion.15, s32[512]{0:T(512)S(1)} %iota_add_fusion.14, s32[2048]{0:T(1024)S(1)} %add_select_fusion.23, pred[2048]{0:T(1024)(128)(4,1)S(1)} %iota_compare_fusion.8, f32[2,4,24,2048]{3,2,1,0:T(8,128)S(1)} %get-tuple-element.938, ...), kind=kOutput, calls=%fused_computation.69.clone.1 | convolution fusion | flops 423362560 | bytes 3356677 | tf_op jit(solution)/shard_map/while/body/eval_jaxpr/ecfm,mj->ecfj/dot_general | solution.py:95
  227.3 20.9 %while.107 = (s32[]{:T(128)}, f32[2,4,48,1024]{3,2,1,0:T(8,128)S(1)}, bf16[2,4,48,1024]{3,2,1,0:T(8,128)(2,1)}, s32[]{:T(128)}, s32[]{:T(128)}, /*index=5*/s32[]{:T(128)}, s32[]{:T(128)}) while((s32[]{:T(128)}, f32[2,4,48,1024]{3,2,1,0:T(8,128)S(1)}, bf16[2,4,48,1024]{3,2,1,0:T(8,128)(2,1)}, s32[]{:T(128)}, s32[]{:T(128)}, ...), condition=%wide.region_4.5_spmd.clone, body=%wide.region_3.4_spmd.clone.sunk | while | flops 413408256 | bytes 3557521 | solution.py:99
  259.8 15.9 %all-reduce.21 = (f32[3,4]{1,0:T(4,128)}, f32[3,4]{1,0:T(4,128)}, f32[3,4]{1,0:T(4,128)}) all-reduce(f32[3,4]{1,0:T(4,128)S(1)} %pad_maximum_fusion.13, f32[3,4]{1,0:T(4,128)S(1)} %pad_maximum_fusion.12, f32[3,4]{1,0:T(4,128)S(1)} %pad_maximum_fusion.11), channel_id=1, replica_groups=mesh['clip'=4,'seg_0'=4,'seg_1'=4,'seg_2'=2,'seg_3'=2] {'seg_0'}, use_global_device_ids=true, to_apply=%region_23.24 | all-reduce | flops 36 | bytes 288 | tf_op jit(solution)/shard_map/psum | solution.py:28
  297.4 20.8 %while.109 = (s32[]{:T(128)}, f32[4,48,1024]{2,1,0:T(8,128)}, bf16[4,48,1024]{2,1,0:T(8,128)(2,1)S(1)}, s32[]{:T(128)}, s32[]{:T(128)}, /*index=5*/s32[]{:T(128)}, s32[]{:T(128)}) while((s32[]{:T(128)}, f32[4,48,1024]{2,1,0:T(8,128)}, bf16[4,48,1024]{2,1,0:T(8,128)(2,1)S(1)}, s32[]{:T(128)}, s32[]{:T(128)}, ...), condition=%wide.region_30.31_spmd.clone, body=%wide.region_29.30_spmd.clone.sunk | while | flops 211688448 | bytes 1782929 | solution.py:99
  325.4 77.4 %while.110 = (s32[]{:T(128)}, f32[4,24,2048]{2,1,0:T(8,128)}, bf16[4,24,2048]{2,1,0:T(8,128)(2,1)S(1)}, s32[]{:T(128)}, s32[]{:T(128)}, /*index=5*/s32[]{:T(128)}, s32[]{:T(128)}) while((s32[]{:T(128)}, f32[4,24,2048]{2,1,0:T(8,128)}, bf16[4,24,2048]{2,1,0:T(8,128)(2,1)S(1)}, s32[]{:T(128)}, s32[]{:T(128)}, ...), condition=%wide.region_32.33_spmd.clone, body=%wide.region_31.32_spmd.clone.sunk | while | flops 221654016 | bytes 1692817 | solution.py:99
  325.7 18.3 %convolution_add_fusion.11 = f32[4,24,2048]{2,1,0:T(8,128)} fusion(f32[2048]{0:T(1024)S(1)} %multiply_subtract_fusion.17, s32[512]{0:T(512)S(1)} %add_select_fusion.25, pred[512]{0:T(512)(128)(4,1)S(1)} %fusion.250, f32[4,24,2048]{2,1,0:T(8,128)} %get-tuple-element.959, pred[]{:T(512)S(6)} %compare.56, ...), kind=kOutput, calls=%fused_computation.130.clone.1 | convolution fusion | flops 221642752 | bytes 1681925 | tf_op jit(solution)/shard_map/while/body/eval_jaxpr/cfj,jm->cfm/dot_general | solution.py:95
  344.1 19.4 %convolution_add_fusion.11 = f32[4,24,2048]{2,1,0:T(8,128)} fusion(f32[2048]{0:T(1024)S(1)} %multiply_subtract_fusion.17, s32[512]{0:T(512)S(1)} %add_select_fusion.25, pred[512]{0:T(512)(128)(4,1)S(1)} %fusion.250, f32[4,24,2048]{2,1,0:T(8,128)} %get-tuple-element.959, pred[]{:T(512)S(6)} %compare.56, ...), kind=kOutput, calls=%fused_computation.130.clone.1 | convolution fusion | flops 221642752 | bytes 1681925 | tf_op jit(solution)/shard_map/while/body/eval_jaxpr/cfj,jm->cfm/dot_general | solution.py:95
  363.6 19.4 %convolution_add_fusion.11 = f32[4,24,2048]{2,1,0:T(8,128)} fusion(f32[2048]{0:T(1024)S(1)} %multiply_subtract_fusion.17, s32[512]{0:T(512)S(1)} %add_select_fusion.25, pred[512]{0:T(512)(128)(4,1)S(1)} %fusion.250, f32[4,24,2048]{2,1,0:T(8,128)} %get-tuple-element.959, pred[]{:T(512)S(6)} %compare.56, ...), kind=kOutput, calls=%fused_computation.130.clone.1 | convolution fusion | flops 221642752 | bytes 1681925 | tf_op jit(solution)/shard_map/while/body/eval_jaxpr/cfj,jm->cfm/dot_general | solution.py:95
  383.1 19.4 %convolution_add_fusion.11 = f32[4,24,2048]{2,1,0:T(8,128)} fusion(f32[2048]{0:T(1024)S(1)} %multiply_subtract_fusion.17, s32[512]{0:T(512)S(1)} %add_select_fusion.25, pred[512]{0:T(512)(128)(4,1)S(1)} %fusion.250, f32[4,24,2048]{2,1,0:T(8,128)} %get-tuple-element.959, pred[]{:T(512)S(6)} %compare.56, ...), kind=kOutput, calls=%fused_computation.130.clone.1 | convolution fusion | flops 221642752 | bytes 1681925 | tf_op jit(solution)/shard_map/while/body/eval_jaxpr/cfj,jm->cfm/dot_general | solution.py:95
  434.8 70.4 %while.111 = (s32[]{:T(128)}, f32[4,2048,24]{1,2,0:T(8,128)S(1)}, bf16[4,24,2048]{2,1,0:T(8,128)(2,1)S(1)}, s32[]{:T(128)}, s32[]{:T(128)}, /*index=5*/s32[]{:T(128)}, s32[]{:T(128)}) while((s32[]{:T(128)}, f32[4,2048,24]{1,2,0:T(8,128)S(1)}, bf16[4,24,2048]{2,1,0:T(8,128)(2,1)S(1)}, s32[]{:T(128)}, s32[]{:T(128)}, ...), condition=%wide.region_34.35_spmd.clone, body=%wide.region_33.34_spmd.clone.sunk | while | flops 221654016 | bytes 1699985 | solution.py:99
  435.1 17.4 %fusion.253 = f32[4,2048,24]{1,2,0:T(8,128)S(1)} fusion(f32[512]{0:T(512)S(1)} %multiply_subtract_fusion.18, s32[512]{0:T(512)S(1)} %iota_add_fusion.15, s32[2048]{0:T(1024)S(1)} %add_select_fusion.26, pred[2048]{0:T(1024)(128)(4,1)S(1)} %iota_compare_fusion.9, f32[4,2048,24]{1,2,0:T(8,128)S(1)} %get-tuple-element.1001, pred[]{:T(512)S(6)} %compare.57, ...), kind=kOutput, calls=%fused_computation.160.clone.1 | convolution fusion | flops 221642752 | bytes 1685509 | tf_op jit(solution)/shard_map/while/body/eval_jaxpr/cfm,mk->ckf/dot_general | solution.py:95
  452.6 17.4 %fusion.253 = f32[4,2048,24]{1,2,0:T(8,128)S(1)} fusion(f32[512]{0:T(512)S(1)} %multiply_subtract_fusion.18, s32[512]{0:T(512)S(1)} %iota_add_fusion.15, s32[2048]{0:T(1024)S(1)} %add_select_fusion.26, pred[2048]{0:T(1024)(128)(4,1)S(1)} %iota_compare_fusion.9, f32[4,2048,24]{1,2,0:T(8,128)S(1)} %get-tuple-element.1001, pred[]{:T(512)S(6)} %compare.57, ...), kind=kOutput, calls=%fused_computation.160.clone.1 | convolution fusion | flops 221642752 | bytes 1685509 | tf_op jit(solution)/shard_map/while/body/eval_jaxpr/cfm,mk->ckf/dot_general | solution.py:95
  470.1 17.4 %fusion.253 = f32[4,2048,24]{1,2,0:T(8,128)S(1)} fusion(f32[512]{0:T(512)S(1)} %multiply_subtract_fusion.18, s32[512]{0:T(512)S(1)} %iota_add_fusion.15, s32[2048]{0:T(1024)S(1)} %add_select_fusion.26, pred[2048]{0:T(1024)(128)(4,1)S(1)} %iota_compare_fusion.9, f32[4,2048,24]{1,2,0:T(8,128)S(1)} %get-tuple-element.1001, pred[]{:T(512)S(6)} %compare.57, ...), kind=kOutput, calls=%fused_computation.160.clone.1 | convolution fusion | flops 221642752 | bytes 1685509 | tf_op jit(solution)/shard_map/while/body/eval_jaxpr/cfm,mk->ckf/dot_general | solution.py:95
  487.6 17.4 %fusion.253 = f32[4,2048,24]{1,2,0:T(8,128)S(1)} fusion(f32[512]{0:T(512)S(1)} %multiply_subtract_fusion.18, s32[512]{0:T(512)S(1)} %iota_add_fusion.15, s32[2048]{0:T(1024)S(1)} %add_select_fusion.26, pred[2048]{0:T(1024)(128)(4,1)S(1)} %iota_compare_fusion.9, f32[4,2048,24]{1,2,0:T(8,128)S(1)} %get-tuple-element.1001, pred[]{:T(512)S(6)} %compare.57, ...), kind=kOutput, calls=%fused_computation.160.clone.1 | convolution fusion | flops 221642752 | bytes 1685509 | tf_op jit(solution)/shard_map/while/body/eval_jaxpr/cfm,mk->ckf/dot_general | solution.py:95
  519.5 18.3 %all-to-all-done.2 = bf16[64,2,1536]{2,1,0:T(2,128)(2,1)S(1)} async-done(((bf16[64,2,1536]{2,1,0:T(2,128)(2,1)}), bf16[64,2,1536]{2,1,0:T(2,128)(2,1)S(1)}, u32[]{:S(2)}, u32[]{:S(2)}) %all-to-all-start.2) | async-done | bytes 393248 | tf_op jit(solution)/shard_map/all_to_all | solution.py:236
  (281 shorter events, 219.0 us)
Async XLA Ops:
  0.6 23.0 %copy-start.19 = (s32[4]{0:T(128)S(1)}, s32[4]{0:T(128)}, u32[]{:S(2)}) copy-start(s32[4]{0:T(128)} %param.17) | copy-start | bytes 52
  8.6 33.4 %all-to-all-start = ((bf16[64,2,1536]{2,1,0:T(2,128)(2,1)}), bf16[64,2,1536]{2,1,0:T(2,128)(2,1)S(1)}, u32[]{:S(2)}, u32[]{:S(2)}) async-start(bf16[64,2,1536]{2,1,0:T(2,128)(2,1)} %reshape.462), calls=%async_computation | async-start | bytes 786432 | tf_op jit(solution)/shard_map/all_to_all | solution.py:128
  24.2 105.7 %copy-start.17 = (s32[4]{0:T(128)}, s32[4]{0:T(128)S(1)}, u32[]{:S(2)}) copy-start(s32[4]{0:T(128)S(1)} %get-tuple-element.765) | copy-start | bytes 52
  47.9 6.5 %copy-start.6 = (f32[4,24,2048]{2,1,0:T(8,128)S(1)}, f32[4,24,2048]{2,1,0:T(8,128)}, u32[]{:S(2)}) copy-start(f32[4,24,2048]{2,1,0:T(8,128)} %custom-call) | copy-start | bytes 2359300
  126.5 3.3 collective-permute-start
  130.1 9.5 %collective-permute-start.1 = (bf16[4,1536]{1,0:T(4,128)(2,1)S(1)}, bf16[4,1536]{1,0:T(4,128)(2,1)S(1)}, u32[]{:S(2)}, u32[]{:S(2)}) collective-permute-start(bf16[4,1536]{1,0:T(4,128)(2,1)S(1)} %slice.297), channel_id=1, source_target_pairs={{1,0},{2,1},{3,2},{4,3},{5,4},{6,5},{7,6},{8,7},{9,8},{10,9},{11,1... | collective-permute-start | bytes 36872 | tf_op jit(solution)/shard_map/ppermute | solution.py:23
  132.5 9.5 %collective-permute-start.2 = (bf16[4,1536]{1,0:T(4,128)(2,1)S(1)}, bf16[4,1536]{1,0:T(4,128)(2,1)S(1)}, u32[]{:S(2)}, u32[]{:S(2)}) collective-permute-start(bf16[4,1536]{1,0:T(4,128)(2,1)S(1)} %slice.303), channel_id=1, source_target_pairs={{1,0},{2,1},{3,2},{4,3},{5,4},{6,5},{7,6},{8,7},{9,8},{10,9},{11,1... | collective-permute-start | bytes 36872 | tf_op jit(solution)/shard_map/ppermute | solution.py:23
  139.6 80.8 %copy-start.14 = (bf16[4,1536]{1,0:T(4,128)(2,1)}, bf16[4,1536]{1,0:T(4,128)(2,1)S(1)}, u32[]{:S(2)}) copy-start(bf16[4,1536]{1,0:T(4,128)(2,1)S(1)} %collective-permute-done.1) | copy-start | bytes 36868
  220.4 29.0 %copy-start = (f32[2,4,24,2048]{3,2,1,0:T(8,128)}, f32[2,4,24,2048]{3,2,1,0:T(8,128)S(1)}, u32[]{:S(2)}) copy-start(f32[2,4,24,2048]{3,2,1,0:T(8,128)S(1)} %get-tuple-element.568) | copy-start | bytes 4718596
  227.3 20.9 %slice-start.1 = ((bf16[4,1536]{1,0:T(4,128)(2,1)}), bf16[4,384]{1,0:T(4,128)(2,1)S(1)}, s32[]{:S(2)}) async-start(bf16[4,1536]{1,0:T(4,128)(2,1)} %copy-done.14), calls=%async_computation.4 | async-start | bytes 6144 | tf_op jit(solution)/shard_map/slice | solution.py:145
  227.3 21.8 %slice-start.2 = ((bf16[4,1536]{1,0:T(4,128)(2,1)}), bf16[4,384]{1,0:T(4,128)(2,1)S(1)}, s32[]{:S(2)}) async-start(bf16[4,1536]{1,0:T(4,128)(2,1)} %copy-done.15), calls=%async_computation.5 | async-start | bytes 6144 | tf_op jit(solution)/shard_map/slice | solution.py:145
  249.2 4.3 copy-start.9
  253.6 4.7 copy-start.27
  253.6 6.1 %copy-start.20 = (s32[4]{0:T(128)S(1)}, s32[4]{0:T(128)}, u32[]{:S(2)}) copy-start(s32[4]{0:T(128)} %param.17) | copy-start | bytes 52
  253.7 42.1 %copy-start.16 = (f32[4]{0:T(128)S(1)}, f32[4]{0:T(128)}, u32[]{:S(2)}) copy-start(f32[4]{0:T(128)} %get-tuple-element.763) | copy-start | bytes 52
  318.1 6.7 %copy-start.1 = (f32[2,4,24,2048]{3,2,1,0:T(8,128)S(1)}, f32[2,4,24,2048]{3,2,1,0:T(8,128)}, u32[]{:S(2)}) copy-start(f32[2,4,24,2048]{3,2,1,0:T(8,128)} %copy-done) | copy-start | bytes 4718596
  412.0 13.6 %slice-start = ((f32[4,51,256]{2,0,1:T(4,128)}), f32[4,48,256]{2,0,1:T(4,128)S(1)}, s32[]{:S(2)}) async-start(f32[4,51,256]{2,0,1:T(4,128)} %pad_add_fusion.2), calls=%async_computation.3 | async-start | bytes 393216 | tf_op jit(solution)/shard_map/slice | solution.py:218
  412.0 13.6 %copy-start.8 = (s32[12288]{0:T(1024)S(1)}, s32[12288]{0:T(1024)}, u32[]{:S(2)}) copy-start(s32[12288]{0:T(1024)} %iota_add_fusion.6) | copy-start | bytes 147460
  412.0 13.5 %copy-start.18 = (s32[4]{0:T(128)S(1)}, s32[4]{0:T(128)}, u32[]{:S(2)}) copy-start(s32[4]{0:T(128)} %copy-done.17) | copy-start | bytes 52
  412.8 22.0 %copy-start.5 = (f32[4,2048,24]{1,2,0:T(8,128)S(1)}, f32[4,2048,24]{1,2,0:T(8,128)}, u32[]{:S(2)}) copy-start(f32[4,2048,24]{1,2,0:T(8,128)} %custom-call.5) | copy-start | bytes 2359300
  413.3 12.3 %collective-permute-start.3 = (f32[4,1536]{1,0:T(4,128)S(1)}, f32[4,1536]{1,0:T(4,128)S(1)}, u32[]{:S(2)}, u32[]{:S(2)}) collective-permute-start(f32[4,1536]{1,0:T(4,128)S(1)} %add_add_fusion.3), channel_id=1, source_target_pairs={{0,1},{1,2},{2,3},{3,4},{4,5},{5,6},{6,7},{7,8},{8,9},{9,10},{10,1... | collective-permute-start | bytes 73736 | tf_op jit(solution)/shard_map/ppermute | solution.py:23
  422.3 88.5 %all-to-all-start.1 = ((f32[4,1,1]{2,1,0:T(1,128)}), f32[4,1,1]{2,1,0:T(1,128)S(1)}, u32[]{:S(2)}, u32[]{:S(2)}) async-start(f32[4,1,1]{2,1,0:T(1,128)} %broadcast_in_dim.314), calls=%async_computation.1 | async-start | bytes 4096 | tf_op jit(solution)/shard_map/all_to_all | solution.py:34
  425.7 9.0 %collective-permute-start.4 = (bf16[4,3,512]{2,1,0:T(4,128)(2,1)S(1)}, bf16[4,3,512]{2,1,0:T(4,128)(2,1)S(1)}, u32[]{:S(2)}, u32[]{:S(2)}) collective-permute-start(bf16[4,3,512]{2,1,0:T(4,128)(2,1)S(1)} %slice.346), channel_id=1, source_target_pairs={{1,0},{2,1},{3,2},{4,3},{5,4},{6,5},{7,6},{8,7},{9,8},{10,9},{11,1... | collective-permute-start | bytes 36872 | tf_op jit(solution)/shard_map/ppermute | solution.py:23
  510.9 26.9 %all-to-all-start.2 = ((bf16[64,2,1536]{2,1,0:T(2,128)(2,1)}), bf16[64,2,1536]{2,1,0:T(2,128)(2,1)S(1)}, u32[]{:S(2)}, u32[]{:S(2)}) async-start(bf16[64,2,1536]{2,1,0:T(2,128)(2,1)} %reshape.464), calls=%async_computation.2 | async-start | bytes 786432 | tf_op jit(solution)/shard_map/all_to_all | solution.py:236
  (19 other events, 66.4 us)
where the time goes:
time: 557 us; the launch traced here: 549 us
  matrix products  340 us (61%)
  local copies, waits for them, and re-layouts  56.7 us (10%)
  waiting for transfers between devices  46.6 us (8%)
  starting transfers between devices  40.3 us (7%)
  blocking collectives  34.2 us (6%)
  other arithmetic  25 us (4%)
    dot_general x22, matrix products, turn(): jnp.einsum(pattern, portion, make_rows(anchor, stride), preferred_element...  340 us
    psum x4, blocking collectives, over_axes(): x = lax.psum(x, axis)  34.2 us
    unnamed x84, local copies, waits for them, and re-layouts  18.5 us
    all_to_all x1, waiting for transfers between devices, body(): lax.all_to_all(rounded, SEG, split_axis=2, concat_axis=3, tiled=True)  18.3 us
    ppermute x5, starting transfers between devices, shifted(): return lax.ppermute(block, axis, route)  15.8 us
    all_to_all x1, waiting for transfers between devices, body(): lax.all_to_all(spectra, SEG, split_axis=3, concat_axis=2, tiled=True)  15.3 us
    all_to_all x1, starting transfers between devices, body(): lax.all_to_all(spectra, SEG, split_axis=3, concat_axis=2, tiled=True)  13.9 us
    ppermute x5, waiting for transfers between devices, shifted(): return lax.ppermute(block, axis, route)  13 us
  transfers between devices with their start and end apart: 8, of which 5 were waited for; matrix products, arithmetic and copies ran while one was open for 15% of the time, Pallas kernels for 0%

commit v1 on v0

--- a/solution.py
+++ b/solution.py
@@ -1,8 +1,9 @@
-from functools import partial
 import math
 
 import jax
 import jax.numpy as jnp
+import ml_dtypes
+import numpy as np
 from jax import lax
 from jax.sharding import Mesh
 from jax.sharding import PartitionSpec as P
@@ -23,12 +24,6 @@
     return lax.ppermute(block, axis, route)
 
 
-def over_axes(x, axes):
-    for axis in axes:
-        x = lax.psum(x, axis)
-    return x
-
-
 def from_everyone(x, axis):
     devices = lax.axis_size(axis)
     return lax.all_to_all(jnp.broadcast_to(x[None], (devices, *x.shape)), axis, 0, 0, tiled=True)
@@ -41,62 +36,23 @@
 def wave_table(bins_index, time_index, points, factor):
     halfway = points // 2
     is_sine = bins_index >= halfway
-    harmonic = jnp.where(is_sine, bins_index - halfway, bins_index)
-    angles = (harmonic * time_index % points).astype(jnp.float32) * (2.0 * math.pi / points)
-    window = 0.5 - 0.5 * jnp.cos(time_index.astype(jnp.float32) * (2.0 * math.pi / points))
-    entry_value = jnp.where(is_sine, -jnp.sin(angles), jnp.cos(angles))
-    return (entry_value * window * factor).astype(jnp.bfloat16)
+    harmonic = np.where(is_sine, bins_index - halfway, bins_index)
+    angles = (harmonic * time_index % points).astype(np.float32) * np.float32(2.0 * math.pi / points)
+    window = np.float32(0.5) - np.float32(0.5) * np.cos(
+        time_index.astype(np.float32) * np.float32(2.0 * math.pi / points)
+    )
+    entry_value = np.where(is_sine, -np.sin(angles), np.cos(angles))
+    return (entry_value * window * np.float32(factor)).astype(ml_dtypes.bfloat16)
 
 
-def analysis_rows(points, anchor, height):
-    time_index = anchor + jnp.arange(height, dtype=jnp.int32)
-    return wave_table(
-        jnp.arange(points, dtype=jnp.int32)[None, :],
-        time_index[:, None],
-        points,
-        1.0 / math.sqrt(points),
-    )
+def analysis_table(points):
+    index = np.arange(points, dtype=np.int32)
+    return wave_table(index[None, :], index[:, None], points, 1.0 / math.sqrt(points))
 
 
-def analysis_cols(points, anchor, height):
-    bins_index = anchor + jnp.arange(height, dtype=jnp.int32)
-    return wave_table(
-        bins_index[:, None],
-        jnp.arange(points, dtype=jnp.int32)[None, :],
-        points,
-        1.0 / math.sqrt(points),
-    )
-
-
-def synth_rows(anchor, height):
-    bins_index = anchor + jnp.arange(height, dtype=jnp.int32)
-    return wave_table(
-        bins_index[:, None], jnp.arange(NFFT, dtype=jnp.int32)[None, :], NFFT, 1.0 / math.sqrt(BINS)
-    )
-
-
-def synth_cols(anchor, height):
-    time_index = anchor + jnp.arange(height, dtype=jnp.int32)
-    return wave_table(
-        jnp.arange(2 * BINS, dtype=jnp.int32)[None, :],
-        time_index[:, None],
-        NFFT,
-        1.0 / math.sqrt(BINS),
-    )
-
-
-def blocked_product(operand, along, make_rows, pattern, out_shape):
-    length_in = operand.shape[along]
-    stride = min(512, length_in)
-
-    def turn(turn_index, summed):
-        anchor = turn_index * stride
-        portion = lax.dynamic_slice_in_dim(operand, anchor, stride, along)
-        return summed + jnp.einsum(
-            pattern, portion, make_rows(anchor, stride), preferred_element_type=jnp.float32
-        )
-
-    return lax.fori_loop(0, length_in // stride, turn, jnp.zeros(out_shape, jnp.float32))
+def synthesis_table():
+    index = np.arange(NFFT, dtype=np.int32)
+    return wave_table(index[:, None], index[None, :], NFFT, 1.0 / math.sqrt(BINS))
 
 
 def spread_parts(quarters):
@@ -127,9 +83,8 @@
     start_sample = seg_index * samples
     block = lax.all_to_all(spectra, SEG, split_axis=3, concat_axis=2, tiled=True)
     stacked = block.reshape(block.shape[0], 2 * BINS, block.shape[3])
-    signals = blocked_product(
-        stacked, 1, synth_rows, "ckf,km->cfm", (block.shape[0], block.shape[3], NFFT)
-    )
+    synthesis = jnp.asarray(synthesis_table())
+    signals = jnp.einsum("ckf,km->cfm", stacked, synthesis, preferred_element_type=jnp.float32)
     spilled = spread_parts(signals.reshape(clip_count, rows_here, 4, HOP))
     spill = shifted(spilled[:, rows_here:], SEG, 1)
     estimate = (
@@ -146,6 +101,7 @@
         for points in sizes_list
     ]
     saved = []
+    tables = []
     spread_list = []
     energy_list = []
     logterm_list = []
@@ -156,12 +112,10 @@
         paired = jnp.stack(
             [framed(est_wave, beyond_pair[0], stride), framed(clean, beyond_pair[1], stride)]
         )
-        spectra_pair = blocked_product(
-            paired,
-            3,
-            partial(analysis_rows, points),
-            "ecfm,mj->ecfj",
-            (2, clip_count, frame_count, points),
+        analysis = jnp.asarray(analysis_table(points))
+        tables.append(analysis)
+        spectra_pair = jnp.einsum(
+            "ecfm,mj->ecfj", paired, analysis, preferred_element_type=jnp.float32
         )
         est_real = spectra_pair[0, :, :, :halfway]
         est_imag = spectra_pair[0, :, :, halfway:]
@@ -184,11 +138,7 @@
     spreads = jnp.stack(spread_list)
     energies = jnp.stack(energy_list)
     logterms = jnp.stack(logterm_list)
-    spreads, energies, logterms = (
-        over_axes(spreads, SEG),
-        over_axes(energies, SEG),
-        over_axes(logterms, SEG),
-    )
+    spreads, energies, logterms = lax.psum(jnp.stack([spreads, energies, logterms]), SEG)
     own_loss = jnp.sum(jnp.sqrt((spreads + EPS_RATIO) / energies) + logterms)
     loss = of_everyone(own_loss, "clip") / (3 * clip_count * lax.axis_size("clip"))
     ratio_weight = 1.0 / jnp.sqrt((spreads + EPS_RATIO) * energies)
@@ -207,12 +157,8 @@
         grad_x = jnp.concatenate(
             [grad_mag * est_real / est_mag, grad_mag * est_imag / est_mag], axis=2
         ).astype(jnp.bfloat16)
-        grad_frames = blocked_product(
-            grad_x,
-            2,
-            partial(analysis_cols, points),
-            "cfj,jm->cfm",
-            (clip_count, frame_count, points),
+        grad_frames = jnp.einsum(
+            "cfj,mj->cfm", grad_x, tables[level], preferred_element_type=jnp.float32
         )
         spread_back = spread_parts(grad_frames.reshape(clip_count, frame_count, 4, stride))
         gradient = gradient + spread_back[:, :frame_count].reshape(clip_count, samples)
@@ -229,8 +175,8 @@
     grad_signals = jnp.concatenate(
         [extended[:, quarter : quarter + rows_here] for quarter in range(4)], axis=2
     )
-    grad_time = blocked_product(
-        grad_signals, 2, synth_cols, "cfm,mk->ckf", (clip_count, 2 * BINS, rows_here)
+    grad_time = jnp.einsum(
+        "cfm,km->ckf", grad_signals, synthesis, preferred_element_type=jnp.float32
     )
     rounded = grad_time.reshape(clip_count, 2, BINS, rows_here).astype(jnp.bfloat16)
     spec_grad = lax.all_to_all(rounded, SEG, split_axis=2, concat_axis=3, tiled=True)

time: 557 us -> 376 us (0.68); the launches traced: 549 us -> 375 us
  matrix products: 340 us -> 27 us
  blocking collectives: 34.2 us -> 200 us
  local copies, waits for them, and re-layouts: 56.7 us -> 44.7 us
  other arithmetic: 25 us -> 13.2 us
    dot_general x22 -> x8, matrix products: 340 us -> 27 us  [the longest x3 8.15 us: body(): jnp.einsum('cfj,mj->cfm', grad_x, tables[level], preferred_element_type=j...]
    psum x4 -> x1, blocking collectives: 34.2 us -> 200 us  [body(): lax.psum(jnp.stack([spreads, energies, logterms]), SEG)]
    reshape x2 -> x0, local copies, waits for them, and re-layouts: 7.03 us -> none  [the longest x1 6.5 us: body(): stacked = block.reshape(block.shape[0], 2 * BINS, block.shape[3])]
    unnamed x84 -> x66, local copies, waits for them, and re-layouts: 18.5 us -> 19.7 us
  transfers between devices with their start and end apart: 8 -> 8, of which waited for: 5 -> 7; matrix products, arithmetic and copies ran while one was open for 15% -> 4% of each run, Pallas kernels for 0% -> 0%
where the time goes in v1:
time: 376 us; the launch traced here: 375 us
  blocking collectives  200 us (53%)
  waiting for transfers between devices  46 us (12%)
  local copies, waits for them, and re-layouts  44.7 us (12%)
  starting transfers between devices  40.4 us (11%)
  matrix products  27 us (7%)
  other arithmetic  13.2 us (4%)
    psum x1, blocking collectives, body(): lax.psum(jnp.stack([spreads, energies, logterms]), SEG)  200 us
    unnamed x66, local copies, waits for them, and re-layouts  19.7 us
    all_to_all x1, waiting for transfers between devices, body(): lax.all_to_all(rounded, SEG, split_axis=2, concat_axis=3, tiled=True)  18.3 us
    all_to_all x1, waiting for transfers between devices, body(): lax.all_to_all(spectra, SEG, split_axis=3, concat_axis=2, tiled=True)  17.1 us
    ppermute x5, starting transfers between devices, shifted(): return lax.ppermute(block, axis, route)  15.5 us
    all_to_all x1, starting transfers between devices, body(): lax.all_to_all(spectra, SEG, split_axis=3, concat_axis=2, tiled=True)  13.9 us
    ppermute x5, waiting for transfers between devices, shifted(): return lax.ppermute(block, axis, route)  10.7 us
    dot_general x3, matrix products, body(): jnp.einsum('cfj,mj->cfm', grad_x, tables[level], preferred_element_type=j...  8.15 us
  transfers between devices with their start and end apart: 8, of which 7 were waited for; matrix products, arithmetic and copies ran while one was open for 4% of the time, Pallas kernels for 0%

profile of v1, /device:TPU:33, one launch (start us, length us, event | category | flops | bytes accessed | tf_op | source)
XLA Modules:
  0.0 375.1 jit_solution(9174423359517544699)
XLA Ops:
  0.6 3.9 %copy.88 = bf16[4,2,16,1536]{2,0,1,3:T(4,128)(2,1)S(1)} copy(bf16[4,2,16,1536]{3,2,1,0:T(8,128)(2,1)} %param.7) | data formatting | bytes 786432 | tf_op args[0]
  4.5 4.1 %reshape.259 = bf16[64,2,1536]{2,1,0:T(2,128)(2,1)} reshape(bf16[1536,2,4,16]{3,2,1,0:T(4,128)(2,1)S(1)} %bitcast.265) | data formatting | bytes 786432
  8.6 13.9 %all-to-all-start = ((bf16[64,2,1536]{2,1,0:T(2,128)(2,1)}), bf16[64,2,1536]{2,1,0:T(2,128)(2,1)S(1)}, u32[]{:S(2)}, u32[]{:S(2)}) async-start(bf16[64,2,1536]{2,1,0:T(2,128)(2,1)} %reshape.259), calls=%async_computation | async-start | bytes 786432 | tf_op jit(solution)/shard_map/all_to_all | solution.py:84
  24.9 17.1 %all-to-all-done = bf16[64,2,1536]{2,1,0:T(2,128)(2,1)S(1)} async-done(((bf16[64,2,1536]{2,1,0:T(2,128)(2,1)}), bf16[64,2,1536]{2,1,0:T(2,128)(2,1)S(1)}, u32[]{:S(2)}, u32[]{:S(2)}) %all-to-all-start) | async-done | bytes 393248 | tf_op jit(solution)/shard_map/all_to_all | solution.py:84
  44.2 2.6 copy.89
  46.8 3.4 reshape.246
  50.3 6.1 %fusion.3 = f32[4,24,4,512]{3,1,0,2:T(8,128)S(1)} fusion(bf16[4,512,2048,1]{2,1,3,0:T(8,128)(2,1)} %constant.159, bf16[4,2048,24]{2,1,0:T(8,128)(2,1)S(1)} %reshape.246), kind=kOutput, calls=%fused_computation.5 | convolution fusion | flops 805306368 | bytes 9568256 | tf_op jit(solution)/shard_map/ckf,km->cfm/dot_general | solution.py:87
  64.2 5.4 %collective-permute-done.1 = bf16[4,1536]{1,0:T(4,128)(2,1)S(1)} collective-permute-done((bf16[4,1536]{1,0:T(4,128)(2,1)S(1)}, bf16[4,1536]{1,0:T(4,128)(2,1)S(1)}, u32[]{:S(2)}, u32[]{:S(2)}) %collective-permute-start.1) | collective-permute-done | bytes 12320 | tf_op jit(solution)/shard_map/ppermute | solution.py:24
  72.5 5.2 %fusion.14 = f32[2,4,24,2048]{3,2,1,0:T(8,128)S(1)} fusion(bf16[2048,2048,1,1]{1,0,3,2:T(8,128)(2,1)} %constant.162, bf16[1,4,24,2048]{3,2,1,0:T(8,128)(2,1)S(1)} %get-tuple-element.85, bf16[1,4,24,2048]{3,2,1,0:T(8,128)(2,1)S(1)} %get-tuple-element.84), kind=kOutput, calls=%fused_computation.15 | convolution fusion | flops 1611005952 | bytes 10747904 | tf_op jit(solution)/shard_map/ecfm,mj->ecfj/dot_general | solution.py:117
  84.8 200.4 %psum.7 = f32[3,3,4]{2,1,0:T(4,128)S(1)} all-reduce(f32[3,3,4]{2,1,0:T(4,128)S(1)} %pad_maximum_fusion.14), channel_id=1, replica_groups=mesh['clip'=4,'seg_0'=4,'seg_1'=4,'seg_2'=2,'seg_3'=2] {'seg_0','seg_1',..., use_global_device_ids=true, to_apply=%region_9.10 | all-reduce | flops 36 | bytes 288 | tf_op jit(solution)/shard_map/psum | solution.py:141
  287.6 6.9 %fusion.37 = f32[4,24,2048]{2,1,0:T(8,128)} fusion(bf16[2048,2048,1]{1,0,2:T(8,128)(2,1)} %constant.165, bf16[4,24,1024]{2,1,0:T(8,128)(2,1)S(1)} %get-tuple-element.22, bf16[4,24,1024]{2,1,0:T(8,128)(2,1)S(1)} %get-tuple-element.21), kind=kOutput, calls=%fused_computation.86 | convolution fusion | flops 806092800 | bytes 9568256 | tf_op jit(solution)/shard_map/cfj,mj->cfm/dot_general | solution.py:160
  294.5 2.6 reshape.234
  297.1 3.1 fusion.57
  308.0 2.6 collective-permute-start.3
  311.9 3.2 all-to-all-start.1
  315.7 6.6 %collective-permute-start.4 = (bf16[4,3,512]{2,1,0:T(4,128)(2,1)S(1)}, bf16[4,3,512]{2,1,0:T(4,128)(2,1)S(1)}, u32[]{:S(2)}, u32[]{:S(2)}) collective-permute-start(bf16[4,3,512]{2,1,0:T(4,128)(2,1)S(1)} %slice.357), channel_id=1, source_target_pairs={{1,0},{2,1},{3,2},{4,3},{5,4},{6,5},{7,6},{8,7},{9,8},{10,9},{11,1... | collective-permute-start | bytes 36872 | tf_op jit(solution)/shard_map/ppermute | solution.py:24
  322.3 2.4 collective-permute-done.4
  324.8 6.0 %fusion = bf16[4,2048,24]{1,2,0:T(8,128)(2,1)S(1)} fusion(bf16[2048,2048,1]{1,0,2:T(8,128)(2,1)} %constant.166, bf16[4,24,512]{2,1,0:T(8,128)(2,1)S(1)} %get-tuple-element.40, bf16[4,24,512]{2,1,0:T(8,128)(2,1)S(1)} %get-tuple-element.41, bf16[4,24,512]{2,1,0:T(8,128)(2,1)S(1)} %get-tuple-element.39, bf16[4,24,512]{2,1,0:T(8,128)(2,1)S(1)} %bitcast.298), kind=kOutput, calls=%fused_computation.1 | convolution fusion | flops 807075840 | bytes 9175040 | tf_op jit(solution)/shard_map/cfm,km->ckf/dot_general | solution.py:178
  332.9 3.5 reshape.261
  336.4 7.8 %all-to-all-start.2 = ((bf16[64,2,1536]{2,1,0:T(2,128)(2,1)}), bf16[64,2,1536]{2,1,0:T(2,128)(2,1)S(1)}, u32[]{:S(2)}, u32[]{:S(2)}) async-start(bf16[64,2,1536]{2,1,0:T(2,128)(2,1)} %reshape.261), calls=%async_computation.2 | async-start | bytes 786432 | tf_op jit(solution)/shard_map/all_to_all | solution.py:182
  345.5 18.3 %all-to-all-done.2 = bf16[64,2,1536]{2,1,0:T(2,128)(2,1)S(1)} async-done(((bf16[64,2,1536]{2,1,0:T(2,128)(2,1)}), bf16[64,2,1536]{2,1,0:T(2,128)(2,1)S(1)}, u32[]{:S(2)}, u32[]{:S(2)}) %all-to-all-start.2) | async-done | bytes 393248 | tf_op jit(solution)/shard_map/all_to_all | solution.py:182
  363.7 3.0 reshape.262
  366.7 2.7 copy.146
  369.4 4.5 %all_to_all.35 = bf16[4,2,16,1536]{3,2,1,0:T(8,128)(2,1)} reshape(bf16[4,2,16,64,24]{4,3,2,1,0:T(8,128)(2,1)} %bitcast.268) | data formatting | bytes 786432 | tf_op jit(solution)/shard_map/all_to_all | solution.py:182
  (148 shorter events, 36.7 us)
Async XLA Ops:
  4.5 18.5 %copy-start.14 = (s32[4]{0:T(128)S(1)}, s32[4]{0:T(128)}, u32[]{:S(2)}) copy-start(s32[4]{0:T(128)} %param.9) | copy-start | bytes 52
  8.6 33.4 %all-to-all-start = ((bf16[64,2,1536]{2,1,0:T(2,128)(2,1)}), bf16[64,2,1536]{2,1,0:T(2,128)(2,1)S(1)}, u32[]{:S(2)}, u32[]{:S(2)}) async-start(bf16[64,2,1536]{2,1,0:T(2,128)(2,1)} %reshape.259), calls=%async_computation | async-start | bytes 786432 | tf_op jit(solution)/shard_map/all_to_all | solution.py:84
  24.2 35.7 %copy-start.12 = (s32[4]{0:T(128)}, s32[4]{0:T(128)S(1)}, u32[]{:S(2)}) copy-start(s32[4]{0:T(128)S(1)} %get-tuple-element.75) | copy-start | bytes 52
  24.3 56.9 %copy-start.15 = (pred[4,48]{1,0:T(4,128)(4,1)}, pred[4,48]{1,0:T(4,128)(4,1)S(1)}, u32[]{:S(2)}) copy-start(pred[4,48]{1,0:T(4,128)(4,1)S(1)} %broadcast_compare_fusion.1) | copy-start | bytes 580
  56.4 3.5 copy-start.7
  56.4 3.5 copy-start.10
  56.4 5.6 %copy-start.20 = (s32[4]{0:T(128)S(1)}, s32[4]{0:T(128)}, u32[]{:S(2)}) copy-start(s32[4]{0:T(128)} %get-tuple-element.76) | copy-start | bytes 52
  56.4 5.6 %copy-start.22 = (s32[96]{0:T(128)S(1)}, s32[96]{0:T(128)}, u32[]{:S(2)}) copy-start(s32[96]{0:T(128)} %iota_add_fusion.3) | copy-start | bytes 1156
  56.5 3.3 collective-permute-start
  60.1 9.5 %collective-permute-start.1 = (bf16[4,1536]{1,0:T(4,128)(2,1)S(1)}, bf16[4,1536]{1,0:T(4,128)(2,1)S(1)}, u32[]{:S(2)}, u32[]{:S(2)}) collective-permute-start(bf16[4,1536]{1,0:T(4,128)(2,1)S(1)} %slice.300), channel_id=1, source_target_pairs={{1,0},{2,1},{3,2},{4,3},{5,4},{6,5},{7,6},{8,7},{9,8},{10,9},{11,1... | collective-permute-start | bytes 36872 | tf_op jit(solution)/shard_map/ppermute | solution.py:24
  62.1 21.3 %copy-start.17 = (pred[4,96]{1,0:T(4,128)(4,1)}, pred[4,96]{1,0:T(4,128)(4,1)S(1)}, u32[]{:S(2)}) copy-start(pred[4,96]{1,0:T(4,128)(4,1)S(1)} %broadcast_compare_fusion.2) | copy-start | bytes 1156
  62.1 9.5 %collective-permute-start.2 = (bf16[4,1536]{1,0:T(4,128)(2,1)S(1)}, bf16[4,1536]{1,0:T(4,128)(2,1)S(1)}, u32[]{:S(2)}, u32[]{:S(2)}) collective-permute-start(bf16[4,1536]{1,0:T(4,128)(2,1)S(1)} %slice.306), channel_id=1, source_target_pairs={{1,0},{2,1},{3,2},{4,3},{5,4},{6,5},{7,6},{8,7},{9,8},{10,9},{11,1... | collective-permute-start | bytes 36872 | tf_op jit(solution)/shard_map/ppermute | solution.py:24
  72.5 5.2 %copy-start.19 = (pred[4,24]{1,0:T(4,128)(4,1)S(1)}, pred[4,24]{1,0:T(4,128)(4,1)}, u32[]{:S(2)}) copy-start(pred[4,24]{1,0:T(4,128)(4,1)} %broadcast_compare_fusion) | copy-start | bytes 292
  77.7 3.5 copy-start
  77.7 2.4 copy-start.21
  300.2 2.0 copy-start.3
  300.6 2.1 copy-start.1
  307.3 8.2 %slice-start = ((f32[4,27,512]{2,0,1:T(4,128)}), f32[4,24,512]{2,0,1:T(4,128)S(1)}, s32[]{:S(2)}) async-start(f32[4,27,512]{2,0,1:T(4,128)} %pad_add_fusion.1), calls=%async_computation.3 | async-start | bytes 393216 | tf_op jit(solution)/shard_map/slice | solution.py:164
  307.3 8.2 %copy-start.8 = (s32[12288]{0:T(1024)S(1)}, s32[12288]{0:T(1024)}, u32[]{:S(2)}) copy-start(s32[12288]{0:T(1024)} %iota_add_fusion) | copy-start | bytes 147460
  307.4 8.2 %copy-start.13 = (s32[4]{0:T(128)S(1)}, s32[4]{0:T(128)}, u32[]{:S(2)}) copy-start(s32[4]{0:T(128)} %copy-done.12) | copy-start | bytes 52
  308.0 7.6 %collective-permute-start.3 = (f32[4,1536]{1,0:T(4,128)S(1)}, f32[4,1536]{1,0:T(4,128)S(1)}, u32[]{:S(2)}, u32[]{:S(2)}) collective-permute-start(f32[4,1536]{1,0:T(4,128)S(1)} %add_add_fusion.3), channel_id=1, source_target_pairs={{0,1},{1,2},{2,3},{3,4},{4,5},{5,6},{6,7},{7,8},{8,9},{9,10},{10,1... | collective-permute-start | bytes 73736 | tf_op jit(solution)/shard_map/ppermute | solution.py:24
  311.9 24.5 %all-to-all-start.1 = ((f32[4,1,1]{2,1,0:T(1,128)}), f32[4,1,1]{2,1,0:T(1,128)S(1)}, u32[]{:S(2)}, u32[]{:S(2)}) async-start(f32[4,1,1]{2,1,0:T(1,128)} %broadcast_in_dim.105), calls=%async_computation.1 | async-start | bytes 4096 | tf_op jit(solution)/shard_map/all_to_all | solution.py:29
  315.7 9.0 %collective-permute-start.4 = (bf16[4,3,512]{2,1,0:T(4,128)(2,1)S(1)}, bf16[4,3,512]{2,1,0:T(4,128)(2,1)S(1)}, u32[]{:S(2)}, u32[]{:S(2)}) collective-permute-start(bf16[4,3,512]{2,1,0:T(4,128)(2,1)S(1)} %slice.357), channel_id=1, source_target_pairs={{1,0},{2,1},{3,2},{4,3},{5,4},{6,5},{7,6},{8,7},{9,8},{10,9},{11,1... | collective-permute-start | bytes 36872 | tf_op jit(solution)/shard_map/ppermute | solution.py:24
  336.4 27.4 %all-to-all-start.2 = ((bf16[64,2,1536]{2,1,0:T(2,128)(2,1)}), bf16[64,2,1536]{2,1,0:T(2,128)(2,1)S(1)}, u32[]{:S(2)}, u32[]{:S(2)}) async-start(bf16[64,2,1536]{2,1,0:T(2,128)(2,1)} %reshape.261), calls=%async_computation.2 | async-start | bytes 786432 | tf_op jit(solution)/shard_map/all_to_all | solution.py:182
  (8 other events, 12.4 us)

commit v2 on v1

v2 whole, which is shorter than its diff:
```python
import math

import jax
import jax.numpy as jnp
import ml_dtypes
import numpy as np
from jax import lax
from jax.experimental import pallas as pl
from jax.experimental.pallas import tpu as pltpu
from jax.sharding import PartitionSpec as P

BINS = 1024
NFFT = 2048
HOP = 512
FRAMES = 1536
CLIPS = 16
SEGS = 64
CLIP_GROUPS = 4
LOCAL_CLIPS = 4
HOPS = 24
ROWS = 128
SLABS = 16
EPS_MAG = 0.1
EPS_RATIO = 1e-05
SIZES = (512, 1024, 2048)
SCALE = float(FRAMES * BINS)
F32 = jnp.float32
BF16 = jnp.bfloat16
MESH = pl.DeviceIdType.MESH


def wave_table(bins_index, time_index, points, factor):
    halfway = points // 2
    is_sine = bins_index >= halfway
    harmonic = np.where(is_sine, bins_index - halfway, bins_index)
    angles = (harmonic * time_index % points).astype(np.float32) * np.float32(2.0 * math.pi / points)
    window = np.float32(0.5) - np.float32(0.5) * np.cos(
        time_index.astype(np.float32) * np.float32(2.0 * math.pi / points)
    )
    entry_value = np.where(is_sine, -np.sin(angles), np.cos(angles))
    return (entry_value * window * np.float32(factor)).astype(ml_dtypes.bfloat16)


def analysis_table(points):
    index = np.arange(points, dtype=np.int32)
    return wave_table(index[None, :], index[:, None], points, 1.0 / math.sqrt(points))


def synthesis_table():
    owner, part, bin_at = np.meshgrid(np.arange(64), np.arange(2), np.arange(16), indexing="ij")
    index = (part * BINS + owner * 16 + bin_at).reshape(-1).astype(np.int32)
    time = np.arange(NFFT, dtype=np.int32)
    return wave_table(index[:, None], time[None, :], NFFT, 1.0 / math.sqrt(BINS))


def to_seg(index):
    return {"seg": index}


def matmul(a, b):
    return lax.dot_general(a, b, (((1,), (0,)), ((), ())), preferred_element_type=F32)


def matmul_nt(a, b):
    return lax.dot_general(a, b, (((1,), (1,)), ((), ())), preferred_element_type=F32)


def swap_lane_groups(tiles):
    lane = lax.broadcasted_iota(jnp.int32, tiles[0].shape, 1) // 32
    results = []
    for j in range(4):
        result = tiles[j]
        for i in range(4):
            if i != j:
                moved = pltpu.roll(tiles[i], (32 * (i - j)) % 128, 1)
                result = jnp.where(lane == i, moved, result)
        results.append(result)
    return results


def overlap_add(windows):
    total = windows[:, :HOP]
    for q in range(1, 4):
        total = total + pltpu.roll(windows[:, q * HOP : (q + 1) * HOP], q, 0)
    return total


def write_windows(windows_ref, wave):
    windows_ref[:, :HOP] = wave.astype(BF16)
    for q in range(1, 4):
        windows_ref[:, q * HOP : (q + 1) * HOP] = pltpu.roll(wave, ROWS - q, 0).astype(BF16)


def fold_rows(tile):
    by_clip = tile.reshape(LOCAL_CLIPS, 4, 8, tile.shape[1]).sum(axis=1)
    return by_clip[:, :, :128] + by_clip[:, :, 128:]


def kernel(
    spec_ref, target_ref, lengths_ref, syn_hbm, a512_hbm, a1024_hbm, a2048_hbm,
    out_ref, loss_ref,
    send_in, recv_in, chunk_in, send_out, recv_out,
    syn, a512, a1024, a2048,
    tgt, tgt_win, est_own, est_tail, est_head, est_win,
    windows, tgt_mag, tgt_log, est_x, mag_part, log_part, grad_x,
    grad_own, grad_tail, grad_head, grad_win,
    sums, stat_send, stat_recv, loss_send, loss_recv,
    table_sem, in_send_sem, in_recv_sem, out_send_sem, out_recv_sem,
    tgt_sem, est_sem, grad_sem, stat_sem, loss_sem,
):
    me = lax.axis_index("seg")
    clip = lax.axis_index("clip")
    after = lax.rem(me + 1, SEGS)
    before = lax.rem(me + SEGS - 1, SEGS)
    analysis = (a512, a1024, a2048)

    barrier = pltpu.get_barrier_semaphore()

    def greet(step, carry):
        pl.semaphore_signal(
            barrier, inc=1, device_id=to_seg(lax.rem(me + step, SEGS)), device_id_type=MESH
        )
        return carry

    lax.fori_loop(1, SEGS, greet, 0)
    for step in range(1, CLIP_GROUPS):
        pl.semaphore_signal(
            barrier,
            inc=1,
            device_id={"clip": lax.rem(clip + step, CLIP_GROUPS)},
            device_id_type=MESH,
        )

    table_copies = [
        pltpu.make_async_copy(source, held, table_sem.at[at])
        for at, (source, held) in enumerate(
            ((a512_hbm, a512), (a1024_hbm, a1024), (a2048_hbm, a2048), (syn_hbm, syn))
        )
    ]
    for copy in table_copies:
        copy.start()

    for part in range(4):
        turned = spec_ref[:, 384 * part : 384 * (part + 1)].astype(F32).T
        send_in[16 * part : 16 * (part + 1)] = turned.reshape(16, HOPS, 128).astype(BF16)
    for hop in range(HOPS):
        tgt[:, hop, :] = target_ref[:, hop * HOP : (hop + 1) * HOP].astype(F32)

    pl.semaphore_wait(barrier, SEGS - 1 + CLIP_GROUPS - 1)

    tgt_copy = pltpu.make_async_remote_copy(
        src_ref=tgt.at[:, pl.ds(0, 8), :],
        dst_ref=tgt.at[:, pl.ds(HOPS, 8), :],
        send_sem=tgt_sem.at[0],
        recv_sem=tgt_sem.at[1],
        device_id=to_seg(before),
        device_id_type=MESH,
    )
    tgt_copy.start()

    my_chunk = me // SLABS

    def send_bins(step, carry):
        there = lax.rem(me + step, SEGS)
        pltpu.make_async_remote_copy(
            src_ref=send_in.at[there],
            dst_ref=recv_in.at[me],
            send_sem=in_send_sem,
            recv_sem=in_recv_sem.at[my_chunk],
            device_id=to_seg(there),
            device_id_type=MESH,
        ).start()
        return carry

    lax.fori_loop(1, SEGS, send_bins, 0)
    pltpu.make_async_copy(send_in.at[me], recv_in.at[me], in_recv_sem.at[my_chunk]).start()

    row = lax.broadcasted_iota(jnp.int32, (ROWS, 1), 0)
    row_clip = row // 32
    row_hop = lax.rem(row, 32)
    row_length = jnp.full((ROWS, 1), lengths_ref[0], jnp.int32)
    for c in range(1, LOCAL_CLIPS):
        row_length = jnp.where(row_clip == c, lengths_ref[c], row_length)
    inside = me * HOPS + row_hop < row_length
    usable = inside & (row_hop < HOPS)

    tgt_copy.wait()
    write_windows(tgt_win, jnp.where(inside, tgt[...].reshape(ROWS, HOP), 0.0))
    for level, points in enumerate(SIZES):
        half = points // 2
        stride = points // 4
        table_copies[level].wait()
        for at in range(HOP // stride):
            rows = pl.ds(at * ROWS, ROWS)

            def target_columns(step, energy, level=level, points=points, half=half, at=at):
                column = pl.multiple_of(step * 256, 256)
                frames = tgt_win[:, at * (points // 4) : at * (points // 4) + points]
                real = matmul(frames, analysis[level][:, pl.ds(column, 256)])
                imag = matmul(frames, analysis[level][:, pl.ds(half + column, 256)])
                power = real * real + imag * imag + EPS_MAG
                place = pl.ds(pl.multiple_of(at * half + column, 256), 256)
                tgt_mag[level, :, place] = jnp.sqrt(power)
                tgt_log[level, :, place] = 0.5 * jnp.log(power)
                return energy + fold_rows(jnp.where(usable, power, 0.0))

            start = jnp.zeros((LOCAL_CLIPS, 8, 128), F32)
            found = lax.fori_loop(0, half // 256, target_columns, start)
            if at == 0:
                sums[3 + level] = found
            else:
                sums[3 + level] = sums[3 + level] + found

    table_copies[3].wait()
    for turn in range(4):
        chunk = lax.rem(my_chunk + (4 - turn), 4)
        slabs = pl.ds(pl.multiple_of(chunk * SLABS, SLABS), SLABS)
        pltpu.make_async_copy(
            send_in.at[slabs], recv_in.at[slabs], in_recv_sem.at[chunk]
        ).wait()
        arrived = recv_in[slabs].astype(F32).reshape(4, 4, HOPS, 128)
        by_source = [arrived[:, i].reshape(4 * HOPS, 128) for i in range(4)]
        by_clip = swap_lane_groups(by_source)
        for c in range(LOCAL_CLIPS):
            for g in range(4):
                block = by_clip[c][g * HOPS : (g + 1) * HOPS]
                block = jnp.concatenate([block, jnp.zeros((8, 128), F32)], axis=0)
                chunk_in[c * 32 : (c + 1) * 32, g * 128 : (g + 1) * 128] = block.astype(BF16)
        for tile in range(4):
            columns = slice(tile * 512, (tile + 1) * 512)
            product = matmul(
                chunk_in[...], syn[pl.ds(pl.multiple_of(chunk * 512, 512), 512), columns]
            )
            if turn == 0:
                windows[:, columns] = product
            else:
                windows[:, columns] = windows[:, columns] + product

    def neighbours(own, tail, head, sem):
        return (
            pltpu.make_async_remote_copy(
                src_ref=own.at[:, pl.ds(HOPS, 8), :],
                dst_ref=tail,
                send_sem=sem.at[0],
                recv_sem=sem.at[1],
                device_id=to_seg(after),
                device_id_type=MESH,
            ),
            pltpu.make_async_remote_copy(
                src_ref=own.at[:, pl.ds(0, 8), :],
                dst_ref=head,
                send_sem=sem.at[2],
                recv_sem=sem.at[3],
                device_id=to_seg(before),
                device_id_type=MESH,
            ),
        )

    def joined(own, tail, head):
        first = jnp.where(me == 0, 0.0, tail[...])
        hop = lax.broadcasted_iota(jnp.int32, head.shape, 1)
        last = jnp.where(hop < 3, head[...], 0.0)
        whole = jnp.concatenate(
            [own[:, :8] + first, own[:, 8:HOPS], own[:, HOPS:] + last], axis=1
        )
        return jnp.where(inside, whole.reshape(ROWS, HOP), 0.0)

    est_own[...] = overlap_add(windows[...]).reshape(LOCAL_CLIPS, 32, HOP)
    est_copies = neighbours(est_own, est_tail, est_head, est_sem)
    for copy in est_copies:
        copy.start()
    for copy in est_copies:
        copy.wait()
    write_windows(est_win, joined(est_own, est_tail, est_head))

    for level, points in enumerate(SIZES):
        half = points // 2
        stride = points // 4
        for at in range(HOP // stride):

            def columns(step, carry, level=level, points=points, half=half, at=at):
                spread, logterm = carry
                column = pl.multiple_of(step * 256, 256)
                frames = est_win[:, at * (points // 4) : at * (points // 4) + points]
                real = matmul(frames, analysis[level][:, pl.ds(column, 256)])
                imag = matmul(frames, analysis[level][:, pl.ds(half + column, 256)])
                power = real * real + imag * imag + EPS_MAG
                inverse = lax.rsqrt(power)
                place = pl.ds(pl.multiple_of(at * half + column, 256), 256)
                gap = power * inverse - tgt_mag[level, :, place]
                log_gap = 0.5 * jnp.log(power) - tgt_log[level, :, place]
                est_x[level, 0, :, place] = real
                est_x[level, 1, :, place] = imag
                mag_part[level, :, place] = gap * inverse
                log_part[level, :, place] = log_gap * inverse * inverse
                return (
                    spread + fold_rows(jnp.where(usable, gap * gap, 0.0)),
                    logterm + fold_rows(jnp.where(usable, log_gap * log_gap, 0.0)),
                )

            start = jnp.zeros((LOCAL_CLIPS, 8, 128), F32)
            spread, logterm = lax.fori_loop(0, half // 256, columns, (start, start))
            if at == 0:
                sums[level] = spread
                sums[6 + level] = logterm
            else:
                sums[level] = sums[level] + spread
                sums[6 + level] = sums[6 + level] + logterm

    flat = sums[...].reshape(36, 8, 128).sum(axis=1)
    flat = jnp.sum(flat, axis=1, keepdims=True)
    lane = lax.broadcasted_iota(jnp.int32, (36, 128), 1)
    line = lax.broadcasted_iota(jnp.int32, (36, 128), 0)
    own_stats = jnp.sum(jnp.where(lane == line, flat, 0.0), axis=0, keepdims=True)
    stat_send[...] = own_stats
    stat_recv[me] = own_stats

    def send_stats(step, carry):
        pltpu.make_async_remote_copy(
            src_ref=stat_send,
            dst_ref=stat_recv.at[me],
            send_sem=stat_sem.at[0],
            recv_sem=stat_sem.at[1],
            device_id=to_seg(lax.rem(me + step, SEGS)),
            device_id_type=MESH,
        ).start()
        return carry

    lax.fori_loop(1, SEGS, send_stats, 0)
    others = stat_recv.at[pl.ds(0, SEGS - 1)]
    pltpu.make_async_copy(others, others, stat_sem.at[1]).wait()
    pltpu.make_async_copy(others, others, stat_sem.at[0]).wait()
    totals = stat_recv[...].sum(axis=0)

    energy = pltpu.roll(totals, 128 - 12, 1)
    logterm = pltpu.roll(totals, 128 - 24, 1)
    place = lax.broadcasted_iota(jnp.int32, (1, 128), 1)
    filled = place < 12
    lane_length = jnp.full((1, 128), lengths_ref[0], jnp.int32)
    for c in range(1, LOCAL_CLIPS):
        lane_length = jnp.where(lax.rem(place, 4) == c, lengths_ref[c], lane_length)
    entries = (lane_length * BINS).astype(F32)
    safe_energy = jnp.where(filled, energy, 1.0)
    safe_spread = jnp.where(filled, totals, 1.0) + EPS_RATIO
    terms = jnp.where(filled, jnp.sqrt(safe_spread / safe_energy) + logterm / entries, 0.0)
    own_loss = jnp.sum(terms, axis=1, keepdims=True) + jnp.zeros((1, 128), F32)
    loss_send[...] = own_loss
    loss_recv[clip] = own_loss
    for step in range(1, CLIP_GROUPS):
        pltpu.make_async_remote_copy(
            src_ref=loss_send,
            dst_ref=loss_recv.at[clip],
            send_sem=loss_sem.at[0],
            recv_sem=loss_sem.at[1],
            device_id={"clip": lax.rem(clip + step, CLIP_GROUPS)},
            device_id_type=MESH,
        ).start()

    weights = SCALE / jnp.sqrt(safe_spread * safe_energy)
    weights = jnp.broadcast_to(weights, (ROWS, 128))
    pick_lane = lax.broadcasted_iota(jnp.int32, (ROWS, 128), 1)
    pick_row = lax.broadcasted_iota(jnp.int32, (ROWS, 128), 0) // 32
    log_weight = (2.0 * SCALE) / (row_length * BINS).astype(F32)
    for level, points in enumerate(SIZES):
        half = points // 2
        mag_weight = jnp.sum(
            jnp.where(pick_lane == level * 4 + pick_row, weights, 0.0), axis=1, keepdims=True
        )
        for at in range(2048 // points):

            def gradients(step, carry, level=level, half=half, at=at, mag_weight=mag_weight):
                column = pl.multiple_of(step * 256, 256)
                place = pl.ds(pl.multiple_of(at * half + column, 256), 256)
                factor = jnp.where(
                    usable,
                    mag_part[level, :, place] * mag_weight + log_part[level, :, place] * log_weight,
                    0.0,
                )
                first = pl.multiple_of(at * 2 * half + column, 256)
                second = pl.multiple_of(at * 2 * half + half + column, 256)
                grad_x[level, :, pl.ds(first, 256)] = (factor * est_x[level, 0, :, place]).astype(BF16)
                grad_x[level, :, pl.ds(second, 256)] = (factor * est_x[level, 1, :, place]).astype(BF16)
                return carry

            lax.fori_loop(0, half // 256, gradients, 0)

    def back(step, carry):
        column = pl.multiple_of(step * 256, 256)
        windows[:, pl.ds(column, 256)] = matmul_nt(grad_x[2], a2048[pl.ds(column, 256), :])
        return carry

    lax.fori_loop(0, 8, back, 0)
    for level, points in ((1, 1024), (0, 512)):
        for at in range(2048 // points):
            for step in range(points // 256):
                first = at * (points // 4) + step * 256
                product = matmul_nt(
                    grad_x[level, :, at * points : (at + 1) * points],
                    analysis[level][step * 256 : (step + 1) * 256, :],
                )
                windows[:, first : first + 256] = windows[:, first : first + 256] + product

    grad_own[...] = overlap_add(windows[...]).reshape(LOCAL_CLIPS, 32, HOP)
    grad_copies = neighbours(grad_own, grad_tail, grad_head, grad_sem)
    for copy in grad_copies:
        copy.start()
    for copy in grad_copies:
        copy.wait()
    write_windows(grad_win, joined(grad_own, grad_tail, grad_head))

    first_tile = me // 8 + 1

    def back_bins(step, carry):
        tile = lax.rem(first_tile + step, 8)
        product = matmul_nt(grad_win[...], syn[pl.ds(pl.multiple_of(tile * 256, 256), 256), :])
        for g in range(2):
            lanes = product[:, g * 128 : (g + 1) * 128]
            by_clip = [lanes[c * 32 : c * 32 + HOPS] for c in range(LOCAL_CLIPS)]
            for i, block in enumerate(swap_lane_groups(by_clip)):
                send_out[tile * 8 + g * 4 + i] = block.astype(BF16)
        for i in range(8):
            there = tile * 8 + i

            @pl.when(there != me)
            def _():
                pltpu.make_async_remote_copy(
                    src_ref=send_out.at[there],
                    dst_ref=recv_out.at[me],
                    send_sem=out_send_sem,
                    recv_sem=out_recv_sem.at[my_chunk],
                    device_id=to_seg(there),
                    device_id_type=MESH,
                ).start()

            @pl.when(there == me)
            def _():
                pltpu.make_async_copy(
                    send_out.at[me], recv_out.at[me], out_recv_sem.at[my_chunk]
                ).start()

        return carry

    lax.fori_loop(0, 8, back_bins, 0)

    three = loss_recv.at[pl.ds(0, CLIP_GROUPS - 1)]
    pltpu.make_async_copy(three, three, loss_sem.at[1]).wait()
    pltpu.make_async_copy(three, three, loss_sem.at[0]).wait()
    loss_ref[...] = loss_recv[...].sum(axis=0) / (3 * CLIPS)

    for chunk in range(4):
        slabs = pl.ds(chunk * SLABS, SLABS)
        pltpu.make_async_copy(
            send_out.at[slabs], recv_out.at[slabs], out_recv_sem.at[chunk]
        ).wait()
        turned = recv_out[slabs].astype(F32).reshape(SLABS * HOPS, 128).T
        out_ref[:, chunk * 384 : (chunk + 1) * 384] = turned.astype(BF16)

    sent = pl.ds(0, SEGS - 1)
    pltpu.make_async_copy(send_in.at[sent], recv_in.at[sent], in_send_sem).wait()
    pltpu.make_async_copy(send_out.at[sent], recv_out.at[sent], out_send_sem).wait()


def body(spectra, target, lengths):
    vmem = pl.BlockSpec(memory_space=pltpu.VMEM)
    smem = pl.BlockSpec(memory_space=pltpu.SMEM)
    anywhere = pl.BlockSpec(memory_space=pl.ANY)
    slabs = pltpu.VMEM((SEGS, HOPS, 128), BF16)
    hops8 = pltpu.VMEM((LOCAL_CLIPS, 8, HOP), F32)
    hops32 = pltpu.VMEM((LOCAL_CLIPS, 32, HOP), F32)
    window = pltpu.VMEM((ROWS, NFFT), BF16)
    entries = pltpu.VMEM((3, ROWS, BINS), F32)
    dma = pltpu.SemaphoreType.DMA
    out, loss = pl.pallas_call(
        kernel,
        out_shape=(
            jax.ShapeDtypeStruct((ROWS, FRAMES), BF16),
            jax.ShapeDtypeStruct((1, 128), F32),
        ),
        in_specs=[vmem, vmem, smem] + [anywhere] * 4,
        out_specs=(vmem, vmem),
        scratch_shapes=[
            slabs, slabs, pltpu.VMEM((ROWS, 512), BF16), slabs, slabs,
            pltpu.VMEM((2048, 2048), BF16), pltpu.VMEM((512, 512), BF16),
            pltpu.VMEM((1024, 1024), BF16), pltpu.VMEM((2048, 2048), BF16),
            hops32, window, hops32, hops8, hops8, window,
            pltpu.VMEM((ROWS, NFFT), F32), entries, entries,
            pltpu.VMEM((3, 2, ROWS, BINS), F32), entries, entries,
            pltpu.VMEM((3, ROWS, NFFT), BF16),
            hops32, hops8, hops8, window,
            pltpu.VMEM((9, LOCAL_CLIPS, 8, 128), F32),
            pltpu.VMEM((1, 128), F32), pltpu.VMEM((SEGS, 1, 128), F32),
            pltpu.VMEM((1, 128), F32), pltpu.VMEM((CLIP_GROUPS, 1, 128), F32),
            dma((4,)), dma, dma((4,)), dma, dma((4,)),
            dma((2,)), dma((4,)), dma((4,)), dma((2,)), dma((2,)),
        ],
        compiler_params=pltpu.CompilerParams(
            collective_id=0, has_side_effects=True, vmem_limit_bytes=60 * 2**20
        ),
        cost_estimate=pl.CostEstimate(
            flops=8 * 10**9, bytes_accessed=20 * 10**6, transcendentals=10**6
        ),
    )(
        spectra.reshape(ROWS, FRAMES),
        target,
        lengths,
        jnp.asarray(synthesis_table()),
        *(jnp.asarray(analysis_table(points)) for points in SIZES),
    )
    return loss[0, 0], out.reshape(LOCAL_CLIPS, 2, BINS // SEGS, FRAMES)


def solution(mesh):
    placed = (P("clip", None, "seg", None), P("clip", "seg"), P("clip"))
    return jax.shard_map(
        body,
        mesh=mesh,
        in_specs=placed,
        out_specs=(P(), P("clip", None, "seg", None)),
        check_vma=False,
    )
```

time: 376 us -> 75.8 us (0.20)
  blocking collectives: 200 us -> 0 us
  Pallas kernels: 0 us -> 71.5 us
  waiting for transfers between devices: 46 us -> 0 us
  local copies, waits for them, and re-layouts: 44.7 us -> 1.77 us
  starting transfers between devices: 40.4 us -> 0 us
  matrix products: 27 us -> 0 us
  other arithmetic: 13.2 us -> 0 us
    psum x1 -> x0, blocking collectives: 200 us -> none  [body(): lax.psum(jnp.stack([spreads, energies, logterms]), SEG)]
    pallas_call x0 -> x1, Pallas kernels: none -> 71.5 us  [body(): pl.pallas_call(kernel, out_shape=(jax.ShapeDtypeStruct((ROWS, FRAMES), BF...]
    all_to_all x3 -> x0, waiting for transfers between devices: 35.3 us -> none  [the longest x1 18.3 us: body(): lax.all_to_all(rounded, SEG, split_axis=2, concat_axis=3, tiled=True)]
    dot_general x8 -> x0, matrix products: 27 us -> none  [the longest x3 8.15 us: body(): jnp.einsum('cfj,mj->cfm', grad_x, tables[level], preferred_element_type=j...]
    all_to_all x3 -> x0, starting transfers between devices: 24.9 us -> none  [the longest x1 13.9 us: body(): lax.all_to_all(spectra, SEG, split_axis=3, concat_axis=2, tiled=True)]
    unnamed x66 -> x1, local copies, waits for them, and re-layouts: 19.7 us -> 1.77 us
    ppermute x5 -> x0, starting transfers between devices: 15.5 us -> none  [shifted(): return lax.ppermute(block, axis, route)]
    ppermute x5 -> x0, waiting for transfers between devices: 10.7 us -> none  [shifted(): return lax.ppermute(block, axis, route)]
  transfers between devices with their start and end apart: 8 -> 0, of which waited for: 7 -> 0; matrix products, arithmetic and copies ran while one was open for 4% -> 0% of each run, Pallas kernels for 0% -> 0%
where the time goes in v2:
time: 75.8 us; the launch traced here: 75.6 us
  Pallas kernels  71.5 us (94%)
  between operations  2.39 us (3%)
  local copies, waits for them, and re-layouts  1.77 us (2%)
    pallas_call x1, Pallas kernels, body(): pl.pallas_call(kernel, out_shape=(jax.ShapeDtypeStruct((ROWS, FRAMES), BF...  71.5 us
    unnamed x1, local copies, waits for them, and re-layouts  1.77 us

profile of v2, /device:TPU:33, one launch (start us, length us, event | category | flops | bytes accessed | tf_op | source)
XLA Modules:
  0.0 75.6 jit_solution(1278139397886173147)
XLA Ops:
  0.6 71.5 %shard_map.86 = (bf16[128,1536]{1,0:T(8,128)(2,1)}, f32[1,128]{1,0:T(1,128)}) custom-call(bf16[128,1536]{1,0:T(8,128)(2,1)} %bitcast.5, bf16[4,12288]{1,0:T(4,128)(2,1)} %target_ref.1, s32[4]{0:T(128)} %lengths_ref.1, bf16[2048,2048]{1,0:T(8,128)(2,1)} %constant.8.clone.syn_hbm, bf16[512,512]{1,0:T(8,128)(2,1)} %constant.9.clone.a512_hbm, ...), custom_call_target="tpu_custom_call" | custom-call | flops 8000000000 | bytes 20000000 | tf_op jit(solution)/shard_map/pallas_call | solution.py:473
  72.7 1.8 %copy.12 = bf16[4,2,16,1536]{3,2,1,0:T(8,128)(2,1)} copy(bf16[4,2,16,1536]{3,2,1,0:T(8,128)(2,1)} %bitcast.4) | data formatting | bytes 786432

commit v3 on v2

--- a/solution.py
+++ b/solution.py
@@ -15,6 +15,7 @@
 FRAMES = 1536
 CLIPS = 16
 SEGS = 64
+WORKS = 32
 CLIP_GROUPS = 4
 LOCAL_CLIPS = 4
 HOPS = 24
@@ -91,6 +92,15 @@
         windows_ref[:, q * HOP : (q + 1) * HOP] = pltpu.roll(wave, ROWS - q, 0).astype(BF16)
 
 
+def halves(first, second):
+    shape = first.shape
+    first, second = first.reshape(-1, 128), second.reshape(-1, 128)
+    low = lax.broadcasted_iota(jnp.int32, first.shape, 1) < 64
+    one = jnp.where(low, first, pltpu.roll(second, 64, 1))
+    other = jnp.where(low, pltpu.roll(first, 64, 1), second)
+    return one.reshape(shape), other.reshape(shape)
+
+
 def fold_rows(tile):
     by_clip = tile.reshape(LOCAL_CLIPS, 4, 8, tile.shape[1]).sum(axis=1)
     return by_clip[:, :, :128] + by_clip[:, :, 128:]
@@ -99,7 +109,7 @@
 def kernel(
     spec_ref, target_ref, lengths_ref, syn_hbm, a512_hbm, a1024_hbm, a2048_hbm,
     out_ref, loss_ref,
-    send_in, recv_in, chunk_in, send_out, recv_out,
+    send_in, recv_in, chunk_in, send_out, recv_out, tgt_rows, tgt_raw, tgt_next,
     syn, a512, a1024, a2048,
     tgt, tgt_win, est_own, est_tail, est_head, est_win,
     windows, tgt_mag, tgt_log, est_x, mag_part, log_part, grad_x,
@@ -110,9 +120,25 @@
 ):
     me = lax.axis_index("seg")
     clip = lax.axis_index("clip")
-    after = lax.rem(me + 1, SEGS)
-    before = lax.rem(me + SEGS - 1, SEGS)
     analysis = (a512, a1024, a2048)
+    spot = me // 4
+    core = lax.rem(me, 2)
+    side = lax.rem(me // 2, 2)
+    work = spot * 2 + core
+
+    def device_of(work_index, side_index):
+        return (work_index // 2) * 4 + side_index * 2 + lax.rem(work_index, 2)
+
+    def slot_of(work_index, side_index):
+        return (work_index // 8) * 16 + side_index * 8 + lax.rem(work_index, 8)
+
+    after = device_of(lax.rem(work + 1, WORKS), side)
+    before = device_of(lax.rem(work + WORKS - 1, WORKS), side)
+    my_slot = slot_of(work, side)
+    loss_peers = [
+        (lax.rem(clip + step // 2, CLIP_GROUPS), device_of(work, lax.rem(side + step, 2)))
+        for step in range(1, 2 * CLIP_GROUPS)
+    ]
 
     barrier = pltpu.get_barrier_semaphore()
 
@@ -123,13 +149,8 @@
         return carry
 
     lax.fori_loop(1, SEGS, greet, 0)
-    for step in range(1, CLIP_GROUPS):
-        pl.semaphore_signal(
-            barrier,
-            inc=1,
-            device_id={"clip": lax.rem(clip + step, CLIP_GROUPS)},
-            device_id_type=MESH,
-        )
+    for peer in loss_peers[1:]:
+        pl.semaphore_signal(barrier, inc=1, device_id=peer, device_id_type=MESH)
 
     table_copies = [
         pltpu.make_async_copy(source, held, table_sem.at[at])
@@ -140,30 +161,79 @@
     for copy in table_copies:
         copy.start()
 
+    for hop in range(HOPS):
+        tgt_rows[:, hop, :] = target_ref[:, hop * HOP : (hop + 1) * HOP].astype(F32)
+    tgt_raw[...] = tgt_rows[...].astype(BF16)
     for part in range(4):
         turned = spec_ref[:, 384 * part : 384 * (part + 1)].astype(F32).T
-        send_in[16 * part : 16 * (part + 1)] = turned.reshape(16, HOPS, 128).astype(BF16)
-    for hop in range(HOPS):
-        tgt[:, hop, :] = target_ref[:, hop * HOP : (hop + 1) * HOP].astype(F32)
-
-    pl.semaphore_wait(barrier, SEGS - 1 + CLIP_GROUPS - 1)
-
-    tgt_copy = pltpu.make_async_remote_copy(
-        src_ref=tgt.at[:, pl.ds(0, 8), :],
-        dst_ref=tgt.at[:, pl.ds(HOPS, 8), :],
+        turned = turned.reshape(8, 2, HOPS, 128)
+        for at, message in enumerate(halves(turned[:, 0], turned[:, 1])):
+            first = part * 16 + at * 8
+            send_in[first : first + 8] = message.astype(BF16)
+
+    pl.semaphore_wait(barrier, SEGS - 1 + len(loss_peers) - 1)
+
+    def hold(to_side):
+        return tgt_raw.at[pl.ds(2 * to_side, 2)], tgt.at[pl.ds(2 * core, 2)]
+
+    across_source, across_place = hold(1 - side)
+    tgt_across = pltpu.make_async_remote_copy(
+        src_ref=across_source,
+        dst_ref=across_place,
         send_sem=tgt_sem.at[0],
         recv_sem=tgt_sem.at[1],
-        device_id=to_seg(before),
+        device_id=to_seg(spot * 4 + (1 - side) * 2 + side),
         device_id_type=MESH,
     )
-    tgt_copy.start()
+    tgt_across.start()
+    near_source, near_place = hold(side)
+    near_stays = core == side
+
+    @pl.when(near_stays)
+    def _():
+        pltpu.make_async_copy(near_source, near_place, tgt_sem.at[1]).start()
+
+    @pl.when(jnp.logical_not(near_stays))
+    def _():
+        pltpu.make_async_remote_copy(
+            src_ref=near_source,
+            dst_ref=near_place,
+            send_sem=tgt_sem.at[2],
+            recv_sem=tgt_sem.at[1],
+            device_id=to_seg(spot * 4 + side * 3),
+            device_id_type=MESH,
+        ).start()
+
+    ahead = lax.rem(spot * 2 + side + WORKS - 1, WORKS)
+    heads = [
+        (tgt_rows.at[pl.ds(2 * to_side, 2), pl.ds(0, 8), :], device_of(ahead, to_side))
+        for to_side in range(2)
+    ]
+    for at, (source, there) in enumerate(heads):
+
+        @pl.when((core == 0) & (there != me))
+        def _(at=at, source=source, there=there):
+            pltpu.make_async_remote_copy(
+                src_ref=source,
+                dst_ref=tgt_next,
+                send_sem=tgt_sem.at[3 + at],
+                recv_sem=tgt_sem.at[5],
+                device_id=to_seg(there),
+                device_id_type=MESH,
+            ).start()
+
+        @pl.when((core == 0) & (there == me))
+        def _(source=source):
+            pltpu.make_async_copy(source, tgt_next, tgt_sem.at[5]).start()
 
     my_chunk = me // SLABS
 
     def send_bins(step, carry):
         there = lax.rem(me + step, SEGS)
         pltpu.make_async_remote_copy(
-            src_ref=send_in.at[there],
+            src_ref=send_in.at[
+                slot_of((there // 4) * 2 + lax.rem(there, 2), lax.rem(there // 2, 2))
+            ],
             dst_ref=recv_in.at[me],
             send_sem=in_send_sem,
             recv_sem=in_recv_sem.at[my_chunk],
@@ -173,43 +243,53 @@
         return carry
 
     lax.fori_loop(1, SEGS, send_bins, 0)
-    pltpu.make_async_copy(send_in.at[me], recv_in.at[me], in_recv_sem.at[my_chunk]).start()
+    pltpu.make_async_copy(send_in.at[my_slot], recv_in.at[me], in_recv_sem.at[my_chunk]).start()
 
     row = lax.broadcasted_iota(jnp.int32, (ROWS, 1), 0)
     row_clip = row // 32
     row_hop = lax.rem(row, 32)
-    row_length = jnp.full((ROWS, 1), lengths_ref[0], jnp.int32)
-    for c in range(1, LOCAL_CLIPS):
-        row_length = jnp.where(row_clip == c, lengths_ref[c], row_length)
-    inside = me * HOPS + row_hop < row_length
+    row_length = jnp.where(
+        lax.rem(row_clip, 2) == 0, lengths_ref[2 * side], lengths_ref[2 * side + 1]
+    )
+    inside = work * (2 * HOPS) + (row_clip // 2) * HOPS + row_hop < row_length
     usable = inside & (row_hop < HOPS)
 
-    tgt_copy.wait()
-    write_windows(tgt_win, jnp.where(inside, tgt[...].reshape(ROWS, HOP), 0.0))
+    pltpu.make_async_copy(tgt_raw, tgt, tgt_sem.at[1]).wait()
+    pltpu.make_async_copy(tgt_next, tgt_next, tgt_sem.at[5]).wait()
+    own = tgt[...].astype(F32)
+    first_half = jnp.concatenate([own[:2], own[2:, :8]], axis=1)
+    second_half = jnp.concatenate([own[2:], tgt_next[...]], axis=1)
+    own = jnp.concatenate([first_half, second_half], axis=0).reshape(ROWS, HOP)
+    write_windows(tgt_win, jnp.where(inside, own, 0.0))
+
+    def frames_of(windows_ref, points):
+        stride = points // 4
+        parts = [
+            windows_ref[:, at * stride : at * stride + points] for at in range(HOP // stride)
+        ]
+        return parts[0] if len(parts) == 1 else jnp.concatenate(parts, axis=0)
+
     for level, points in enumerate(SIZES):
         half = points // 2
-        stride = points // 4
+        count = NFFT // points
         table_copies[level].wait()
-        for at in range(HOP // stride):
-            rows = pl.ds(at * ROWS, ROWS)
-
-            def target_columns(step, energy, level=level, points=points, half=half, at=at):
-                column = pl.multiple_of(step * 256, 256)
-                frames = tgt_win[:, at * (points // 4) : at * (points // 4) + points]
-                real = matmul(frames, analysis[level][:, pl.ds(column, 256)])
-                imag = matmul(frames, analysis[level][:, pl.ds(half + column, 256)])
-                power = real * real + imag * imag + EPS_MAG
+
+        def target_columns(step, energy, level=level, points=points, half=half, count=count):
+            column = pl.multiple_of(step * 256, 256)
+            frames = frames_of(tgt_win, points)
+            real = matmul(frames, analysis[level][:, pl.ds(column, 256)])
+            imag = matmul(frames, analysis[level][:, pl.ds(half + column, 256)])
+            power = real * real + imag * imag + EPS_MAG
+            for at in range(count):
                 place = pl.ds(pl.multiple_of(at * half + column, 256), 256)
-                tgt_mag[level, :, place] = jnp.sqrt(power)
-                tgt_log[level, :, place] = 0.5 * jnp.log(power)
-                return energy + fold_rows(jnp.where(usable, power, 0.0))
-
-            start = jnp.zeros((LOCAL_CLIPS, 8, 128), F32)
-            found = lax.fori_loop(0, half // 256, target_columns, start)
-            if at == 0:
-                sums[3 + level] = found
-            else:
-                sums[3 + level] = sums[3 + level] + found
+                part = power[at * ROWS : (at + 1) * ROWS]
+                tgt_mag[level, :, place] = jnp.sqrt(part)
+                tgt_log[level, :, place] = 0.5 * jnp.log(part)
+                energy = energy + fold_rows(jnp.where(usable, part, 0.0))
+            return energy
+
+        start = jnp.zeros((LOCAL_CLIPS, 8, 128), F32)
+        sums[3 + level] = lax.fori_loop(0, half // 256, target_columns, start)
 
     table_copies[3].wait()
     for turn in range(4):
@@ -239,7 +319,7 @@
     def neighbours(own, tail, head, sem):
         return (
             pltpu.make_async_remote_copy(
-                src_ref=own.at[:, pl.ds(HOPS, 8), :],
+                src_ref=own.at[pl.ds(2, 2), pl.ds(HOPS, 8), :],
                 dst_ref=tail,
                 send_sem=sem.at[0],
                 recv_sem=sem.at[1],
@@ -247,7 +327,7 @@
                 device_id_type=MESH,
             ),
             pltpu.make_async_remote_copy(
-                src_ref=own.at[:, pl.ds(0, 8), :],
+                src_ref=own.at[pl.ds(0, 2), pl.ds(0, 8), :],
                 dst_ref=head,
                 send_sem=sem.at[2],
                 recv_sem=sem.at[3],
@@ -257,12 +337,17 @@
         )
 
     def joined(own, tail, head):
-        first = jnp.where(me == 0, 0.0, tail[...])
+        before_us = jnp.where(work == 0, 0.0, tail[...])
         hop = lax.broadcasted_iota(jnp.int32, head.shape, 1)
-        last = jnp.where(hop < 3, head[...], 0.0)
-        whole = jnp.concatenate(
-            [own[:, :8] + first, own[:, 8:HOPS], own[:, HOPS:] + last], axis=1
+        after_us = jnp.where(hop < 3, head[...], 0.0)
+        one, two = own[:2], own[2:]
+        spill = one[:, HOPS:]
+        middle = jnp.where(hop < 3, spill + two[:, :8], 0.0)
+        one = jnp.concatenate([one[:, :8] + before_us, one[:, 8:HOPS], middle], axis=1)
+        two = jnp.concatenate(
+            [two[:, :8] + spill, two[:, 8:HOPS], two[:, HOPS:] + after_us], axis=1
         )
+        whole = jnp.concatenate([one, two], axis=0)
         return jnp.where(inside, whole.reshape(ROWS, HOP), 0.0)
 
     est_own[...] = overlap_add(windows[...]).reshape(LOCAL_CLIPS, 32, HOP)
@@ -270,42 +355,34 @@
     for copy in est_copies:
         copy.start()
     for copy in est_copies:
-        copy.wait()
+        copy.wait_recv()
     write_windows(est_win, joined(est_own, est_tail, est_head))
 
     for level, points in enumerate(SIZES):
         half = points // 2
-        stride = points // 4
-        for at in range(HOP // stride):
-
-            def columns(step, carry, level=level, points=points, half=half, at=at):
-                spread, logterm = carry
-                column = pl.multiple_of(step * 256, 256)
-                frames = est_win[:, at * (points // 4) : at * (points // 4) + points]
-                real = matmul(frames, analysis[level][:, pl.ds(column, 256)])
-                imag = matmul(frames, analysis[level][:, pl.ds(half + column, 256)])
+        count = NFFT // points
+        spread = jnp.zeros((LOCAL_CLIPS, 8, 128), F32)
+        logterm = jnp.zeros((LOCAL_CLIPS, 8, 128), F32)
+        for column in range(0, half, 256):
+            frames = frames_of(est_win, points)
+            all_real = matmul(frames, analysis[level][:, column : column + 256])
+            all_imag = matmul(frames, analysis[level][:, half + column : half + column + 256])
+            for at in range(count):
+                rows = slice(at * ROWS, (at + 1) * ROWS)
+                real, imag = all_real[rows], all_imag[rows]
                 power = real * real + imag * imag + EPS_MAG
                 inverse = lax.rsqrt(power)
-                place = pl.ds(pl.multiple_of(at * half + column, 256), 256)
+                place = slice(at * half + column, at * half + column + 256)
                 gap = power * inverse - tgt_mag[level, :, place]
                 log_gap = 0.5 * jnp.log(power) - tgt_log[level, :, place]
                 est_x[level, 0, :, place] = real
                 est_x[level, 1, :, place] = imag
                 mag_part[level, :, place] = gap * inverse
                 log_part[level, :, place] = log_gap * inverse * inverse
-                return (
-                    spread + fold_rows(jnp.where(usable, gap * gap, 0.0)),
-                    logterm + fold_rows(jnp.where(usable, log_gap * log_gap, 0.0)),
-                )
-
-            start = jnp.zeros((LOCAL_CLIPS, 8, 128), F32)
-            spread, logterm = lax.fori_loop(0, half // 256, columns, (start, start))
-            if at == 0:
-                sums[level] = spread
-                sums[6 + level] = logterm
-            else:
-                sums[level] = sums[level] + spread
-                sums[6 + level] = sums[6 + level] + logterm
+                spread = spread + fold_rows(jnp.where(usable, gap * gap, 0.0))
+                logterm = logterm + fold_rows(jnp.where(usable, log_gap * log_gap, 0.0))
+        sums[level] = spread
+        sums[6 + level] = logterm
 
     flat = sums[...].reshape(36, 8, 128).sum(axis=1)
     flat = jnp.sum(flat, axis=1, keepdims=True)
@@ -313,46 +390,48 @@
     line = lax.broadcasted_iota(jnp.int32, (36, 128), 0)
     own_stats = jnp.sum(jnp.where(lane == line, flat, 0.0), axis=0, keepdims=True)
     stat_send[...] = own_stats
-    stat_recv[me] = own_stats
+    stat_recv[work] = own_stats
 
     def send_stats(step, carry):
         pltpu.make_async_remote_copy(
             src_ref=stat_send,
-            dst_ref=stat_recv.at[me],
+            dst_ref=stat_recv.at[work],
             send_sem=stat_sem.at[0],
             recv_sem=stat_sem.at[1],
-            device_id=to_seg(lax.rem(me + step, SEGS)),
+            device_id=to_seg(device_of(lax.rem(work + step, WORKS), side)),
             device_id_type=MESH,
         ).start()
         return carry
 
-    lax.fori_loop(1, SEGS, send_stats, 0)
-    others = stat_recv.at[pl.ds(0, SEGS - 1)]
+    lax.fori_loop(1, WORKS, send_stats, 0)
+    others = stat_recv.at[pl.ds(0, WORKS - 1)]
     pltpu.make_async_copy(others, others, stat_sem.at[1]).wait()
-    pltpu.make_async_copy(others, others, stat_sem.at[0]).wait()
     totals = stat_recv[...].sum(axis=0)
 
+    place = lax.broadcasted_iota(jnp.int32, (1, 128), 1)
+    low_half = lax.rem(place, 4) < 2
+    totals = totals + jnp.where(low_half, pltpu.roll(totals, 126, 1), pltpu.roll(totals, 2, 1))
     energy = pltpu.roll(totals, 128 - 12, 1)
     logterm = pltpu.roll(totals, 128 - 24, 1)
-    place = lax.broadcasted_iota(jnp.int32, (1, 128), 1)
     filled = place < 12
-    lane_length = jnp.full((1, 128), lengths_ref[0], jnp.int32)
-    for c in range(1, LOCAL_CLIPS):
-        lane_length = jnp.where(lax.rem(place, 4) == c, lengths_ref[c], lane_length)
+    lane_length = jnp.where(
+        lax.rem(place, 2) == 0, lengths_ref[2 * side], lengths_ref[2 * side + 1]
+    )
     entries = (lane_length * BINS).astype(F32)
     safe_energy = jnp.where(filled, energy, 1.0)
     safe_spread = jnp.where(filled, totals, 1.0) + EPS_RATIO
-    terms = jnp.where(filled, jnp.sqrt(safe_spread / safe_energy) + logterm / entries, 0.0)
+    terms = jnp.where(filled & low_half, jnp.sqrt(safe_spread / safe_energy) + logterm / entries, 0.0)
     own_loss = jnp.sum(terms, axis=1, keepdims=True) + jnp.zeros((1, 128), F32)
     loss_send[...] = own_loss
-    loss_recv[clip] = own_loss
-    for step in range(1, CLIP_GROUPS):
+    my_loss = clip * 2 + side
+    loss_recv[my_loss] = own_loss
+    for peer in loss_peers:
         pltpu.make_async_remote_copy(
             src_ref=loss_send,
-            dst_ref=loss_recv.at[clip],
+            dst_ref=loss_recv.at[my_loss],
             send_sem=loss_sem.at[0],
             recv_sem=loss_sem.at[1],
-            device_id={"clip": lax.rem(clip + step, CLIP_GROUPS)},
+            device_id=peer,
             device_id_type=MESH,
         ).start()
 
@@ -384,28 +463,27 @@
 
             lax.fori_loop(0, half // 256, gradients, 0)
 
-    def back(step, carry):
-        column = pl.multiple_of(step * 256, 256)
-        windows[:, pl.ds(column, 256)] = matmul_nt(grad_x[2], a2048[pl.ds(column, 256), :])
-        return carry
-
-    lax.fori_loop(0, 8, back, 0)
+    for step in range(0, NFFT, 256):
+        windows[:, step : step + 256] = matmul_nt(grad_x[2], a2048[step : step + 256, :])
     for level, points in ((1, 1024), (0, 512)):
-        for at in range(2048 // points):
-            for step in range(points // 256):
-                first = at * (points // 4) + step * 256
-                product = matmul_nt(
-                    grad_x[level, :, at * points : (at + 1) * points],
-                    analysis[level][step * 256 : (step + 1) * 256, :],
+        count = NFFT // points
+        stacked = jnp.concatenate(
+            [grad_x[level, :, at * points : (at + 1) * points] for at in range(count)], axis=0
+        )
+        for step in range(0, points, 256):
+            product = matmul_nt(stacked, analysis[level][step : step + 256, :])
+            for at in range(count):
+                first = at * (points // 4) + step
+                windows[:, first : first + 256] = (
+                    windows[:, first : first + 256] + product[at * ROWS : (at + 1) * ROWS]
                 )
-                windows[:, first : first + 256] = windows[:, first : first + 256] + product
 
     grad_own[...] = overlap_add(windows[...]).reshape(LOCAL_CLIPS, 32, HOP)
     grad_copies = neighbours(grad_own, grad_tail, grad_head, grad_sem)
     for copy in grad_copies:
         copy.start()
     for copy in grad_copies:
-        copy.wait()
+        copy.wait_recv()
     write_windows(grad_win, joined(grad_own, grad_tail, grad_head))
 
     first_tile = me // 8 + 1
@@ -425,7 +503,7 @@
             def _():
                 pltpu.make_async_remote_copy(
                     src_ref=send_out.at[there],
-                    dst_ref=recv_out.at[me],
+                    dst_ref=recv_out.at[my_slot],
                     send_sem=out_send_sem,
                     recv_sem=out_recv_sem.at[my_chunk],
                     device_id=to_seg(there),
@@ -435,16 +513,15 @@
             @pl.when(there == me)
             def _():
                 pltpu.make_async_copy(
-                    send_out.at[me], recv_out.at[me], out_recv_sem.at[my_chunk]
+                    send_out.at[me], recv_out.at[my_slot], out_recv_sem.at[my_chunk]
                 ).start()
 
         return carry
 
     lax.fori_loop(0, 8, back_bins, 0)
 
-    three = loss_recv.at[pl.ds(0, CLIP_GROUPS - 1)]
-    pltpu.make_async_copy(three, three, loss_sem.at[1]).wait()
-    pltpu.make_async_copy(three, three, loss_sem.at[0]).wait()
+    seven = loss_recv.at[pl.ds(0, 2 * CLIP_GROUPS - 1)]
+    pltpu.make_async_copy(seven, seven, loss_sem.at[1]).wait()
     loss_ref[...] = loss_recv[...].sum(axis=0) / (3 * CLIPS)
 
     for chunk in range(4):
@@ -452,9 +529,27 @@
         pltpu.make_async_copy(
             send_out.at[slabs], recv_out.at[slabs], out_recv_sem.at[chunk]
         ).wait()
-        turned = recv_out[slabs].astype(F32).reshape(SLABS * HOPS, 128).T
+        arrived = recv_out[slabs].astype(F32)
+        one, two = halves(arrived[:8], arrived[8:])
+        whole = jnp.concatenate([one[:, None], two[:, None]], axis=1)
+        turned = whole.reshape(SLABS * HOPS, 128).T
         out_ref[:, chunk * 384 : (chunk + 1) * 384] = turned.astype(BF16)
 
+    for copy in est_copies + grad_copies + (tgt_across,):
+        copy.wait_send()
+
+    @pl.when(jnp.logical_not(near_stays))
+    def _():
+        pltpu.make_async_copy(near_source, near_source, tgt_sem.at[2]).wait()
+
+    for at, (source, there) in enumerate(heads):
+
+        @pl.when((core == 0) & (there != me))
+        def _(at=at):
+            pltpu.make_async_copy(tgt_next, tgt_next, tgt_sem.at[3 + at]).wait()
+
+    pltpu.make_async_copy(others, others, stat_sem.at[0]).wait()
+    pltpu.make_async_copy(seven, seven, loss_sem.at[0]).wait()
     sent = pl.ds(0, SEGS - 1)
     pltpu.make_async_copy(send_in.at[sent], recv_in.at[sent], in_send_sem).wait()
     pltpu.make_async_copy(send_out.at[sent], recv_out.at[sent], out_send_sem).wait()
@@ -465,7 +560,8 @@
     smem = pl.BlockSpec(memory_space=pltpu.SMEM)
     anywhere = pl.BlockSpec(memory_space=pl.ANY)
     slabs = pltpu.VMEM((SEGS, HOPS, 128), BF16)
-    hops8 = pltpu.VMEM((LOCAL_CLIPS, 8, HOP), F32)
+    hops8 = pltpu.VMEM((2, 8, HOP), F32)
+    hops24 = pltpu.VMEM((LOCAL_CLIPS, HOPS, HOP), BF16)
     hops32 = pltpu.VMEM((LOCAL_CLIPS, 32, HOP), F32)
     window = pltpu.VMEM((ROWS, NFFT), BF16)
     entries = pltpu.VMEM((3, ROWS, BINS), F32)
@@ -480,18 +576,19 @@
         out_specs=(vmem, vmem),
         scratch_shapes=[
             slabs, slabs, pltpu.VMEM((ROWS, 512), BF16), slabs, slabs,
+            pltpu.VMEM((LOCAL_CLIPS, HOPS, HOP), F32), hops24, hops8,
             pltpu.VMEM((2048, 2048), BF16), pltpu.VMEM((512, 512), BF16),
             pltpu.VMEM((1024, 1024), BF16), pltpu.VMEM((2048, 2048), BF16),
-            hops32, window, hops32, hops8, hops8, window,
+            hops24, window, hops32, hops8, hops8, window,
             pltpu.VMEM((ROWS, NFFT), F32), entries, entries,
             pltpu.VMEM((3, 2, ROWS, BINS), F32), entries, entries,
             pltpu.VMEM((3, ROWS, NFFT), BF16),
             hops32, hops8, hops8, window,
             pltpu.VMEM((9, LOCAL_CLIPS, 8, 128), F32),
-            pltpu.VMEM((1, 128), F32), pltpu.VMEM((SEGS, 1, 128), F32),
-            pltpu.VMEM((1, 128), F32), pltpu.VMEM((CLIP_GROUPS, 1, 128), F32),
+            pltpu.VMEM((1, 128), F32), pltpu.VMEM((WORKS, 1, 128), F32),
+            pltpu.VMEM((1, 128), F32), pltpu.VMEM((2 * CLIP_GROUPS, 1, 128), F32),
             dma((4,)), dma, dma((4,)), dma, dma((4,)),
-            dma((2,)), dma((4,)), dma((4,)), dma((2,)), dma((2,)),
+            dma((6,)), dma((4,)), dma((4,)), dma((2,)), dma((2,)),
         ],
         compiler_params=pltpu.CompilerParams(
             collective_id=0, has_side_effects=True, vmem_limit_bytes=60 * 2**20

time: 75.8 us -> 68.3 us (0.901)
  Pallas kernels: 71.5 us -> 63.5 us
    pallas_call x1, Pallas kernels: 71.5 us -> 63.5 us  [body(): pl.pallas_call(kernel, out_shape=(jax.ShapeDtypeStruct((ROWS, FRAMES), BF...]
where the time goes in v3:
time: 68.3 us; the launch traced here: 67.7 us
  Pallas kernels  63.5 us (93%)
  between operations  2.39 us (3%)
  local copies, waits for them, and re-layouts  1.77 us (3%)
    pallas_call x1, Pallas kernels, body(): pl.pallas_call(kernel, out_shape=(jax.ShapeDtypeStruct((ROWS, FRAMES), BF...  63.5 us
    unnamed x1, local copies, waits for them, and re-layouts  1.77 us

profile of v3, /device:TPU:33, one launch (start us, length us, event | category | flops | bytes accessed | tf_op | source)
XLA Modules:
  0.0 67.7 jit_solution(16946977392942381619)
XLA Ops:
  0.6 63.5 %shard_map.86 = (bf16[128,1536]{1,0:T(8,128)(2,1)}, f32[1,128]{1,0:T(1,128)}) custom-call(bf16[128,1536]{1,0:T(8,128)(2,1)} %bitcast.5, bf16[4,12288]{1,0:T(4,128)(2,1)} %target_ref.1, s32[4]{0:T(128)} %lengths_ref.1, bf16[2048,2048]{1,0:T(8,128)(2,1)} %constant.8.clone.syn_hbm, bf16[512,512]{1,0:T(8,128)(2,1)} %constant.9.clone.a512_hbm, ...), custom_call_target="tpu_custom_call" | custom-call | flops 8000000000 | bytes 20000000 | tf_op jit(solution)/shard_map/pallas_call | solution.py:569
  64.8 1.8 %copy.12 = bf16[4,2,16,1536]{3,2,1,0:T(8,128)(2,1)} copy(bf16[4,2,16,1536]{3,2,1,0:T(8,128)(2,1)} %bitcast.4) | data formatting | bytes 786432

commit v4 on v3

--- a/solution.py
+++ b/solution.py
@@ -79,10 +79,10 @@
     return results
 
 
-def overlap_add(windows):
-    total = windows[:, :HOP]
-    for q in range(1, 4):
-        total = total + pltpu.roll(windows[:, q * HOP : (q + 1) * HOP], q, 0)
+def overlap_add(windows_ref, quarters=4):
+    total = windows_ref[:, :HOP]
+    for q in range(1, quarters):
+        total = total + pltpu.roll(windows_ref[:, q * HOP : (q + 1) * HOP], q, 0)
     return total
 
 
@@ -112,8 +112,8 @@
     send_in, recv_in, chunk_in, send_out, recv_out, tgt_rows, tgt_raw, tgt_next,
     syn, a512, a1024, a2048,
     tgt, tgt_win, est_own, est_tail, est_head, est_win,
-    windows, tgt_mag, tgt_log, est_x, mag_part, log_part, grad_x,
-    grad_own, grad_tail, grad_head, grad_win,
+    windows, mag_windows, tgt_mag, tgt_log, grad_x,
+    grad_own, tail_send, head_send, grad_tail, grad_head, grad_win,
     sums, stat_send, stat_recv, loss_send, loss_recv,
     table_sem, in_send_sem, in_recv_sem, out_send_sem, out_recv_sem,
     tgt_sem, est_sem, grad_sem, stat_sem, loss_sem,
@@ -253,6 +253,9 @@
     )
     inside = work * (2 * HOPS) + (row_clip // 2) * HOPS + row_hop < row_length
     usable = inside & (row_hop < HOPS)
+    log_weight = (2.0 * SCALE) / (row_length * BINS).astype(F32)
+    for level in range(2):
+        mag_windows[level] = jnp.zeros((ROWS, NFFT), F32)
 
     pltpu.make_async_copy(tgt_raw, tgt, tgt_sem.at[1]).wait()
     pltpu.make_async_copy(tgt_next, tgt_next, tgt_sem.at[5]).wait()
@@ -316,10 +319,10 @@
             else:
                 windows[:, columns] = windows[:, columns] + product
 
-    def neighbours(own, tail, head, sem):
+    def neighbours(tail_source, tail, head_source, head, sem):
         return (
             pltpu.make_async_remote_copy(
-                src_ref=own.at[pl.ds(2, 2), pl.ds(HOPS, 8), :],
+                src_ref=tail_source,
                 dst_ref=tail,
                 send_sem=sem.at[0],
                 recv_sem=sem.at[1],
@@ -327,7 +330,7 @@
                 device_id_type=MESH,
             ),
             pltpu.make_async_remote_copy(
-                src_ref=own.at[pl.ds(0, 2), pl.ds(0, 8), :],
+                src_ref=head_source,
                 dst_ref=head,
                 send_sem=sem.at[2],
                 recv_sem=sem.at[3],
@@ -337,9 +340,9 @@
         )
 
     def joined(own, tail, head):
-        before_us = jnp.where(work == 0, 0.0, tail[...])
+        before_us = jnp.where(work == 0, 0.0, tail)
         hop = lax.broadcasted_iota(jnp.int32, head.shape, 1)
-        after_us = jnp.where(hop < 3, head[...], 0.0)
+        after_us = jnp.where(hop < 3, head, 0.0)
         one, two = own[:2], own[2:]
         spill = one[:, HOPS:]
         middle = jnp.where(hop < 3, spill + two[:, :8], 0.0)
@@ -350,13 +353,19 @@
         whole = jnp.concatenate([one, two], axis=0)
         return jnp.where(inside, whole.reshape(ROWS, HOP), 0.0)
 
-    est_own[...] = overlap_add(windows[...]).reshape(LOCAL_CLIPS, 32, HOP)
-    est_copies = neighbours(est_own, est_tail, est_head, est_sem)
+    est_own[...] = overlap_add(windows).reshape(LOCAL_CLIPS, 32, HOP)
+    est_copies = neighbours(
+        est_own.at[pl.ds(2, 2), pl.ds(HOPS, 8), :],
+        est_tail,
+        est_own.at[pl.ds(0, 2), pl.ds(0, 8), :],
+        est_head,
+        est_sem,
+    )
     for copy in est_copies:
         copy.start()
     for copy in est_copies:
         copy.wait_recv()
-    write_windows(est_win, joined(est_own, est_tail, est_head))
+    write_windows(est_win, joined(est_own[...], est_tail[...], est_head[...]))
 
     for level, points in enumerate(SIZES):
         half = points // 2
@@ -375,10 +384,15 @@
                 place = slice(at * half + column, at * half + column + 256)
                 gap = power * inverse - tgt_mag[level, :, place]
                 log_gap = 0.5 * jnp.log(power) - tgt_log[level, :, place]
-                est_x[level, 0, :, place] = real
-                est_x[level, 1, :, place] = imag
-                mag_part[level, :, place] = gap * inverse
-                log_part[level, :, place] = log_gap * inverse * inverse
+                mag_factor = jnp.where(usable, gap * inverse, 0.0)
+                log_factor = jnp.where(usable, log_gap * inverse * inverse * log_weight, 0.0)
+                for part, first in (
+                    (real, at * points + column),
+                    (imag, at * points + half + column),
+                ):
+                    lanes = slice(first, first + 256)
+                    grad_x[level, :ROWS, lanes] = (mag_factor * part).astype(BF16)
+                    grad_x[level, ROWS:, lanes] = (log_factor * part).astype(BF16)
                 spread = spread + fold_rows(jnp.where(usable, gap * gap, 0.0))
                 logterm = logterm + fold_rows(jnp.where(usable, log_gap * log_gap, 0.0))
         sums[level] = spread
@@ -404,6 +418,41 @@
         return carry
 
     lax.fori_loop(1, WORKS, send_stats, 0)
+    def add_to(ref, first, product):
+        ref[:, first : first + 256] = ref[:, first : first + 256] + product
+
+    for step in range(0, NFFT, 256):
+        product = matmul_nt(grad_x[2], a2048[step : step + 256, :])
+        mag_windows[2, :, step : step + 256] = product[:ROWS]
+        windows[:, step : step + 256] = product[ROWS:]
+    for level, points in ((1, 1024), (0, 512)):
+        count = NFFT // points
+        stacked = jnp.concatenate(
+            [grad_x[level, :, at * points : (at + 1) * points] for at in range(count)], axis=0
+        )
+        for step in range(0, points, 256):
+            product = matmul_nt(stacked, analysis[level][step : step + 256, :])
+            for at in range(count):
+                first = at * (points // 4) + step
+                base = at * 2 * ROWS
+                add_to(mag_windows.at[level], first, product[base : base + ROWS])
+                add_to(windows, first, product[base + ROWS : base + 2 * ROWS])
+
+    for level in range(3):
+        grad_own[level] = overlap_add(mag_windows.at[level], level + 2)
+    grad_own[3] = overlap_add(windows)
+    hop8 = lax.broadcasted_iota(jnp.int32, (2, 8, HOP), 1)
+    for pair in range(2):
+        upper = grad_own[2 * pair].reshape(LOCAL_CLIPS, 32, HOP)
+        lower = grad_own[2 * pair + 1].reshape(LOCAL_CLIPS, 32, HOP)
+        tail_send[pair] = jnp.where(
+            hop8 < 4, upper[2:, HOPS:], pltpu.roll(lower[2:, HOPS:], 4, 1)
+        )
+        head_send[pair] = jnp.where(hop8 < 4, upper[:2, :8], pltpu.roll(lower[:2, :8], 4, 1))
+    grad_copies = neighbours(tail_send, grad_tail, head_send, grad_head, grad_sem)
+    for copy in grad_copies:
+        copy.start()
+
     others = stat_recv.at[pl.ds(0, WORKS - 1)]
     pltpu.make_async_copy(others, others, stat_sem.at[1]).wait()
     totals = stat_recv[...].sum(axis=0)
@@ -421,6 +470,70 @@
     safe_energy = jnp.where(filled, energy, 1.0)
     safe_spread = jnp.where(filled, totals, 1.0) + EPS_RATIO
     terms = jnp.where(filled & low_half, jnp.sqrt(safe_spread / safe_energy) + logterm / entries, 0.0)
+    weights = SCALE / jnp.sqrt(safe_spread * safe_energy)
+    weights = jnp.broadcast_to(weights, (ROWS, 128))
+    pick_lane = lax.broadcasted_iota(jnp.int32, (ROWS, 128), 1)
+    pick_row = lax.broadcasted_iota(jnp.int32, (ROWS, 128), 0) // 32
+    mag_weights = [
+        jnp.sum(jnp.where(pick_lane == level * 4 + pick_row, weights, 0.0), axis=1, keepdims=True)
+        for level in range(3)
+    ]
+    own = grad_own[3]
+    for level in range(3):
+        own = own + mag_weights[level] * grad_own[level]
+    for copy in grad_copies:
+        copy.wait_recv()
+
+    def weighted(received):
+        def row_of(component):
+            block = received[component // 2]
+            return block if component % 2 == 0 else pltpu.roll(block, 4, 1)
+
+        total = row_of(3)
+        for level in range(3):
+            weight = mag_weights[level].reshape(LOCAL_CLIPS, 32, 1)[:2, :8]
+            total = total + weight * row_of(level)
+        return jnp.where(hop8 < 3, total, 0.0)
+
+    write_windows(
+        grad_win,
+        joined(own.reshape(LOCAL_CLIPS, 32, HOP), weighted(grad_tail), weighted(grad_head)),
+    )
+
+    first_tile = me // 8 + 1
+
+    def back_bins(step, carry):
+        tile = lax.rem(first_tile + step, 8)
+        product = matmul_nt(grad_win[...], syn[pl.ds(pl.multiple_of(tile * 256, 256), 256), :])
+        for g in range(2):
+            lanes = product[:, g * 128 : (g + 1) * 128]
+            by_clip = [lanes[c * 32 : c * 32 + HOPS] for c in range(LOCAL_CLIPS)]
+            for i, block in enumerate(swap_lane_groups(by_clip)):
+                send_out[tile * 8 + g * 4 + i] = block.astype(BF16)
+        for i in range(8):
+            there = tile * 8 + i
+
+            @pl.when(there != me)
+            def _():
+                pltpu.make_async_remote_copy(
+                    src_ref=send_out.at[there],
+                    dst_ref=recv_out.at[my_slot],
+                    send_sem=out_send_sem,
+                    recv_sem=out_recv_sem.at[my_chunk],
+                    device_id=to_seg(there),
+                    device_id_type=MESH,
+                ).start()
+
+            @pl.when(there == me)
+            def _():
+                pltpu.make_async_copy(
+                    send_out.at[me], recv_out.at[my_slot], out_recv_sem.at[my_chunk]
+                ).start()
+
+        return carry
+
+    lax.fori_loop(0, 8, back_bins, 0)
+
     own_loss = jnp.sum(terms, axis=1, keepdims=True) + jnp.zeros((1, 128), F32)
     loss_send[...] = own_loss
     my_loss = clip * 2 + side
@@ -435,91 +548,6 @@
             device_id_type=MESH,
         ).start()
 
-    weights = SCALE / jnp.sqrt(safe_spread * safe_energy)
-    weights = jnp.broadcast_to(weights, (ROWS, 128))
-    pick_lane = lax.broadcasted_iota(jnp.int32, (ROWS, 128), 1)
-    pick_row = lax.broadcasted_iota(jnp.int32, (ROWS, 128), 0) // 32
-    log_weight = (2.0 * SCALE) / (row_length * BINS).astype(F32)
-    for level, points in enumerate(SIZES):
-        half = points // 2
-        mag_weight = jnp.sum(
-            jnp.where(pick_lane == level * 4 + pick_row, weights, 0.0), axis=1, keepdims=True
-        )
-        for at in range(2048 // points):
-
-            def gradients(step, carry, level=level, half=half, at=at, mag_weight=mag_weight):
-                column = pl.multiple_of(step * 256, 256)
-                place = pl.ds(pl.multiple_of(at * half + column, 256), 256)
-                factor = jnp.where(
-                    usable,
-                    mag_part[level, :, place] * mag_weight + log_part[level, :, place] * log_weight,
-                    0.0,
-                )
-                first = pl.multiple_of(at * 2 * half + column, 256)
-                second = pl.multiple_of(at * 2 * half + half + column, 256)
-                grad_x[level, :, pl.ds(first, 256)] = (factor * est_x[level, 0, :, place]).astype(BF16)
-                grad_x[level, :, pl.ds(second, 256)] = (factor * est_x[level, 1, :, place]).astype(BF16)
-                return carry
-
-            lax.fori_loop(0, half // 256, gradients, 0)
-
-    for step in range(0, NFFT, 256):
-        windows[:, step : step + 256] = matmul_nt(grad_x[2], a2048[step : step + 256, :])
-    for level, points in ((1, 1024), (0, 512)):
-        count = NFFT // points
-        stacked = jnp.concatenate(
-            [grad_x[level, :, at * points : (at + 1) * points] for at in range(count)], axis=0
-        )
-        for step in range(0, points, 256):
-            product = matmul_nt(stacked, analysis[level][step : step + 256, :])
-            for at in range(count):
-                first = at * (points // 4) + step
-                windows[:, first : first + 256] = (
-                    windows[:, first : first + 256] + product[at * ROWS : (at + 1) * ROWS]
-                )
-
-    grad_own[...] = overlap_add(windows[...]).reshape(LOCAL_CLIPS, 32, HOP)
-    grad_copies = neighbours(grad_own, grad_tail, grad_head, grad_sem)
-    for copy in grad_copies:
-        copy.start()
-    for copy in grad_copies:
-        copy.wait_recv()
-    write_windows(grad_win, joined(grad_own, grad_tail, grad_head))
-
-    first_tile = me // 8 + 1
-
-    def back_bins(step, carry):
-        tile = lax.rem(first_tile + step, 8)
-        product = matmul_nt(grad_win[...], syn[pl.ds(pl.multiple_of(tile * 256, 256), 256), :])
-        for g in range(2):
-            lanes = product[:, g * 128 : (g + 1) * 128]
-            by_clip = [lanes[c * 32 : c * 32 + HOPS] for c in range(LOCAL_CLIPS)]
-            for i, block in enumerate(swap_lane_groups(by_clip)):
-                send_out[tile * 8 + g * 4 + i] = block.astype(BF16)
-        for i in range(8):
-            there = tile * 8 + i
-
-            @pl.when(there != me)
-            def _():
-                pltpu.make_async_remote_copy(
-                    src_ref=send_out.at[there],
-                    dst_ref=recv_out.at[my_slot],
-                    send_sem=out_send_sem,
-                    recv_sem=out_recv_sem.at[my_chunk],
-                    device_id=to_seg(there),
-                    device_id_type=MESH,
-                ).start()
-
-            @pl.when(there == me)
-            def _():
-                pltpu.make_async_copy(
-                    send_out.at[me], recv_out.at[my_slot], out_recv_sem.at[my_chunk]
-                ).start()
-
-        return carry
-
-    lax.fori_loop(0, 8, back_bins, 0)
-
     seven = loss_recv.at[pl.ds(0, 2 * CLIP_GROUPS - 1)]
     pltpu.make_async_copy(seven, seven, loss_sem.at[1]).wait()
     loss_ref[...] = loss_recv[...].sum(axis=0) / (3 * CLIPS)
@@ -560,6 +588,7 @@
     smem = pl.BlockSpec(memory_space=pltpu.SMEM)
     anywhere = pl.BlockSpec(memory_space=pl.ANY)
     slabs = pltpu.VMEM((SEGS, HOPS, 128), BF16)
+    pairs = pltpu.VMEM((2, 2, 8, HOP), F32)
     hops8 = pltpu.VMEM((2, 8, HOP), F32)
     hops24 = pltpu.VMEM((LOCAL_CLIPS, HOPS, HOP), BF16)
     hops32 = pltpu.VMEM((LOCAL_CLIPS, 32, HOP), F32)
@@ -580,10 +609,9 @@
             pltpu.VMEM((2048, 2048), BF16), pltpu.VMEM((512, 512), BF16),
             pltpu.VMEM((1024, 1024), BF16), pltpu.VMEM((2048, 2048), BF16),
             hops24, window, hops32, hops8, hops8, window,
-            pltpu.VMEM((ROWS, NFFT), F32), entries, entries,
-            pltpu.VMEM((3, 2, ROWS, BINS), F32), entries, entries,
-            pltpu.VMEM((3, ROWS, NFFT), BF16),
-            hops32, hops8, hops8, window,
+            pltpu.VMEM((ROWS, NFFT), F32), pltpu.VMEM((3, ROWS, NFFT), F32), entries, entries,
+            pltpu.VMEM((3, 2 * ROWS, NFFT), BF16),
+            pltpu.VMEM((4, ROWS, HOP), F32), pairs, pairs, pairs, pairs, window,
             pltpu.VMEM((9, LOCAL_CLIPS, 8, 128), F32),
             pltpu.VMEM((1, 128), F32), pltpu.VMEM((WORKS, 1, 128), F32),
             pltpu.VMEM((1, 128), F32), pltpu.VMEM((2 * CLIP_GROUPS, 1, 128), F32),

time: 68.3 us -> 63.7 us (0.933)
  Pallas kernels: 63.5 us -> 59.3 us
    pallas_call x1, Pallas kernels: 63.5 us -> 59.3 us  [body(): pl.pallas_call(kernel, out_shape=(jax.ShapeDtypeStruct((ROWS, FRAMES), BF...]
where the time goes in v4:
time: 63.7 us; the launch traced here: 63.5 us
  Pallas kernels  59.3 us (93%)
  between operations  2.39 us (4%)
  local copies, waits for them, and re-layouts  1.77 us (3%)
    pallas_call x1, Pallas kernels, body(): pl.pallas_call(kernel, out_shape=(jax.ShapeDtypeStruct((ROWS, FRAMES), BF...  59.3 us
    unnamed x1, local copies, waits for them, and re-layouts  1.77 us

profile of v4, /device:TPU:33, one launch (start us, length us, event | category | flops | bytes accessed | tf_op | source)
XLA Modules:
  0.0 63.5 jit_solution(2495160148317548761)
XLA Ops:
  0.6 59.3 %shard_map.86 = (bf16[128,1536]{1,0:T(8,128)(2,1)}, f32[1,128]{1,0:T(1,128)}) custom-call(bf16[128,1536]{1,0:T(8,128)(2,1)} %bitcast.5, bf16[4,12288]{1,0:T(4,128)(2,1)} %target_ref.1, s32[4]{0:T(128)} %lengths_ref.1, bf16[2048,2048]{1,0:T(8,128)(2,1)} %constant.8.clone.syn_hbm, bf16[512,512]{1,0:T(8,128)(2,1)} %constant.9.clone.a512_hbm, ...), custom_call_target="tpu_custom_call" | custom-call | flops 8000000000 | bytes 20000000 | tf_op jit(solution)/shard_map/pallas_call | solution.py:598
  60.6 1.8 %copy.12 = bf16[4,2,16,1536]{3,2,1,0:T(8,128)(2,1)} copy(bf16[4,2,16,1536]{3,2,1,0:T(8,128)(2,1)} %bitcast.4) | data formatting | bytes 786432

commit v5 on v4

--- a/solution.py
+++ b/solution.py
@@ -173,59 +173,6 @@
 
     pl.semaphore_wait(barrier, SEGS - 1 + len(loss_peers) - 1)
 
-    def hold(to_side):
-        return tgt_raw.at[pl.ds(2 * to_side, 2)], tgt.at[pl.ds(2 * core, 2)]
-
-    across_source, across_place = hold(1 - side)
-    tgt_across = pltpu.make_async_remote_copy(
-        src_ref=across_source,
-        dst_ref=across_place,
-        send_sem=tgt_sem.at[0],
-        recv_sem=tgt_sem.at[1],
-        device_id=to_seg(spot * 4 + (1 - side) * 2 + side),
-        device_id_type=MESH,
-    )
-    tgt_across.start()
-    near_source, near_place = hold(side)
-    near_stays = core == side
-
-    @pl.when(near_stays)
-    def _():
-        pltpu.make_async_copy(near_source, near_place, tgt_sem.at[1]).start()
-
-    @pl.when(jnp.logical_not(near_stays))
-    def _():
-        pltpu.make_async_remote_copy(
-            src_ref=near_source,
-            dst_ref=near_place,
-            send_sem=tgt_sem.at[2],
-            recv_sem=tgt_sem.at[1],
-            device_id=to_seg(spot * 4 + side * 3),
-            device_id_type=MESH,
-        ).start()
-
-    ahead = lax.rem(spot * 2 + side + WORKS - 1, WORKS)
-    heads = [
-        (tgt_rows.at[pl.ds(2 * to_side, 2), pl.ds(0, 8), :], device_of(ahead, to_side))
-        for to_side in range(2)
-    ]
-    for at, (source, there) in enumerate(heads):
-
-        @pl.when((core == 0) & (there != me))
-        def _(at=at, source=source, there=there):
-            pltpu.make_async_remote_copy(
-                src_ref=source,
-                dst_ref=tgt_next,
-                send_sem=tgt_sem.at[3 + at],
-                recv_sem=tgt_sem.at[5],
-                device_id=to_seg(there),
-                device_id_type=MESH,
-            ).start()
-
-        @pl.when((core == 0) & (there == me))
-        def _(source=source):
-            pltpu.make_async_copy(source, tgt_next, tgt_sem.at[5]).start()
-
     my_chunk = me // SLABS
 
     def send_bins(step, carry):
@@ -245,6 +192,59 @@
     lax.fori_loop(1, SEGS, send_bins, 0)
     pltpu.make_async_copy(send_in.at[my_slot], recv_in.at[me], in_recv_sem.at[my_chunk]).start()
 
+    def hold(to_side):
+        return tgt_raw.at[pl.ds(2 * to_side, 2)], tgt.at[pl.ds(2 * core, 2)]
+
+    across_source, across_place = hold(1 - side)
+    tgt_across = pltpu.make_async_remote_copy(
+        src_ref=across_source,
+        dst_ref=across_place,
+        send_sem=tgt_sem.at[0],
+        recv_sem=tgt_sem.at[1],
+        device_id=to_seg(spot * 4 + (1 - side) * 2 + side),
+        device_id_type=MESH,
+    )
+    tgt_across.start()
+    near_source, near_place = hold(side)
+    near_stays = core == side
+
+    @pl.when(near_stays)
+    def _():
+        pltpu.make_async_copy(near_source, near_place, tgt_sem.at[1]).start()
+
+    @pl.when(jnp.logical_not(near_stays))
+    def _():
+        pltpu.make_async_remote_copy(
+            src_ref=near_source,
+            dst_ref=near_place,
+            send_sem=tgt_sem.at[2],
+            recv_sem=tgt_sem.at[1],
+            device_id=to_seg(spot * 4 + side * 3),
+            device_id_type=MESH,
+        ).start()
+
+    ahead = lax.rem(spot * 2 + side + WORKS - 1, WORKS)
+    heads = [
+        (tgt_rows.at[pl.ds(2 * to_side, 2), pl.ds(0, 8), :], device_of(ahead, to_side))
+        for to_side in range(2)
+    ]
+    for at, (source, there) in enumerate(heads):
+
+        @pl.when((core == 0) & (there != me))
+        def _(at=at, source=source, there=there):
+            pltpu.make_async_remote_copy(
+                src_ref=source,
+                dst_ref=tgt_next,
+                send_sem=tgt_sem.at[3 + at],
+                recv_sem=tgt_sem.at[5],
+                device_id=to_seg(there),
+                device_id_type=MESH,
+            ).start()
+
+        @pl.when((core == 0) & (there == me))
+        def _(source=source):
+            pltpu.make_async_copy(source, tgt_next, tgt_sem.at[5]).start()
+
     row = lax.broadcasted_iota(jnp.int32, (ROWS, 1), 0)
     row_clip = row // 32
     row_hop = lax.rem(row, 32)
@@ -257,46 +257,9 @@
     for level in range(2):
         mag_windows[level] = jnp.zeros((ROWS, NFFT), F32)
 
-    pltpu.make_async_copy(tgt_raw, tgt, tgt_sem.at[1]).wait()
-    pltpu.make_async_copy(tgt_next, tgt_next, tgt_sem.at[5]).wait()
-    own = tgt[...].astype(F32)
-    first_half = jnp.concatenate([own[:2], own[2:, :8]], axis=1)
-    second_half = jnp.concatenate([own[2:], tgt_next[...]], axis=1)
-    own = jnp.concatenate([first_half, second_half], axis=0).reshape(ROWS, HOP)
-    write_windows(tgt_win, jnp.where(inside, own, 0.0))
-
-    def frames_of(windows_ref, points):
-        stride = points // 4
-        parts = [
-            windows_ref[:, at * stride : at * stride + points] for at in range(HOP // stride)
-        ]
-        return parts[0] if len(parts) == 1 else jnp.concatenate(parts, axis=0)
-
-    for level, points in enumerate(SIZES):
-        half = points // 2
-        count = NFFT // points
-        table_copies[level].wait()
-
-        def target_columns(step, energy, level=level, points=points, half=half, count=count):
-            column = pl.multiple_of(step * 256, 256)
-            frames = frames_of(tgt_win, points)
-            real = matmul(frames, analysis[level][:, pl.ds(column, 256)])
-            imag = matmul(frames, analysis[level][:, pl.ds(half + column, 256)])
-            power = real * real + imag * imag + EPS_MAG
-            for at in range(count):
-                place = pl.ds(pl.multiple_of(at * half + column, 256), 256)
-                part = power[at * ROWS : (at + 1) * ROWS]
-                tgt_mag[level, :, place] = jnp.sqrt(part)
-                tgt_log[level, :, place] = 0.5 * jnp.log(part)
-                energy = energy + fold_rows(jnp.where(usable, part, 0.0))
-            return energy
-
-        start = jnp.zeros((LOCAL_CLIPS, 8, 128), F32)
-        sums[3 + level] = lax.fori_loop(0, half // 256, target_columns, start)
-
     table_copies[3].wait()
     for turn in range(4):
-        chunk = lax.rem(my_chunk + (4 - turn), 4)
+        chunk = lax.rem(my_chunk + (3 - turn), 4)
         slabs = pl.ds(pl.multiple_of(chunk * SLABS, SLABS), SLABS)
         pltpu.make_async_copy(
             send_in.at[slabs], recv_in.at[slabs], in_recv_sem.at[chunk]
@@ -363,6 +326,44 @@
     )
     for copy in est_copies:
         copy.start()
+
+    pltpu.make_async_copy(tgt_raw, tgt, tgt_sem.at[1]).wait()
+    pltpu.make_async_copy(tgt_next, tgt_next, tgt_sem.at[5]).wait()
+    own = tgt[...].astype(F32)
+    first_half = jnp.concatenate([own[:2], own[2:, :8]], axis=1)
+    second_half = jnp.concatenate([own[2:], tgt_next[...]], axis=1)
+    own = jnp.concatenate([first_half, second_half], axis=0).reshape(ROWS, HOP)
+    write_windows(tgt_win, jnp.where(inside, own, 0.0))
+
+    def frames_of(windows_ref, points):
+        stride = points // 4
+        parts = [
+            windows_ref[:, at * stride : at * stride + points] for at in range(HOP // stride)
+        ]
+        return parts[0] if len(parts) == 1 else jnp.concatenate(parts, axis=0)
+
+    for level, points in enumerate(SIZES):
+        half = points // 2
+        count = NFFT // points
+        table_copies[level].wait()
+
+        def target_columns(step, energy, level=level, points=points, half=half, count=count):
+            column = pl.multiple_of(step * 256, 256)
+            frames = frames_of(tgt_win, points)
+            real = matmul(frames, analysis[level][:, pl.ds(column, 256)])
+            imag = matmul(frames, analysis[level][:, pl.ds(half + column, 256)])
+            power = real * real + imag * imag + EPS_MAG
+            for at in range(count):
+                place = pl.ds(pl.multiple_of(at * half + column, 256), 256)
+                part = power[at * ROWS : (at + 1) * ROWS]
+                tgt_mag[level, :, place] = jnp.sqrt(part)
+                tgt_log[level, :, place] = 0.5 * jnp.log(part)
+                energy = energy + fold_rows(jnp.where(usable, part, 0.0))
+            return energy
+
+        start = jnp.zeros((LOCAL_CLIPS, 8, 128), F32)
+        sums[3 + level] = lax.fori_loop(0, half // 256, target_columns, start)
+
     for copy in est_copies:
         copy.wait_recv()
     write_windows(est_win, joined(est_own[...], est_tail[...], est_head[...]))
@@ -552,8 +553,9 @@
     pltpu.make_async_copy(seven, seven, loss_sem.at[1]).wait()
     loss_ref[...] = loss_recv[...].sum(axis=0) / (3 * CLIPS)
 
-    for chunk in range(4):
-        slabs = pl.ds(chunk * SLABS, SLABS)
+    for turn in range(4):
+        chunk = lax.rem(my_chunk + (3 - turn), 4)
+        slabs = pl.ds(pl.multiple_of(chunk * SLABS, SLABS), SLABS)
         pltpu.make_async_copy(
             send_out.at[slabs], recv_out.at[slabs], out_recv_sem.at[chunk]
         ).wait()
@@ -561,7 +563,7 @@
         one, two = halves(arrived[:8], arrived[8:])
         whole = jnp.concatenate([one[:, None], two[:, None]], axis=1)
         turned = whole.reshape(SLABS * HOPS, 128).T
-        out_ref[:, chunk * 384 : (chunk + 1) * 384] = turned.astype(BF16)
+        out_ref[:, pl.ds(pl.multiple_of(chunk * 384, 128), 384)] = turned.astype(BF16)
 
     for copy in est_copies + grad_copies + (tgt_across,):
         copy.wait_send()

time: 63.7 us -> 62.7 us (0.984)
  Pallas kernels: 59.3 us -> 58 us
    pallas_call x1, Pallas kernels: 59.3 us -> 58 us  [body(): pl.pallas_call(kernel, out_shape=(jax.ShapeDtypeStruct((ROWS, FRAMES), BF...]
where the time goes in v5:
time: 62.7 us; the launch traced here: 62.1 us
  Pallas kernels  58 us (93%)
  between operations  2.39 us (4%)
  local copies, waits for them, and re-layouts  1.77 us (3%)
    pallas_call x1, Pallas kernels, body(): pl.pallas_call(kernel, out_shape=(jax.ShapeDtypeStruct((ROWS, FRAMES), BF...  58 us
    unnamed x1, local copies, waits for them, and re-layouts  1.77 us

profile of v5, /device:TPU:33, one launch (start us, length us, event | category | flops | bytes accessed | tf_op | source)
XLA Modules:
  0.0 62.1 jit_solution(8161292381108064902)
XLA Ops:
  0.6 58.0 %shard_map.86 = (bf16[128,1536]{1,0:T(8,128)(2,1)}, f32[1,128]{1,0:T(1,128)}) custom-call(bf16[128,1536]{1,0:T(8,128)(2,1)} %bitcast.5, bf16[4,12288]{1,0:T(4,128)(2,1)} %target_ref.1, s32[4]{0:T(128)} %lengths_ref.1, bf16[2048,2048]{1,0:T(8,128)(2,1)} %constant.8.clone.syn_hbm, bf16[512,512]{1,0:T(8,128)(2,1)} %constant.9.clone.a512_hbm, ...), custom_call_target="tpu_custom_call" | custom-call | flops 8000000000 | bytes 20000000 | tf_op jit(solution)/shard_map/pallas_call | solution.py:600
  59.2 1.8 %copy.12 = bf16[4,2,16,1536]{3,2,1,0:T(8,128)(2,1)} copy(bf16[4,2,16,1536]{3,2,1,0:T(8,128)(2,1)} %bitcast.4) | data formatting | bytes 786432

commit v6 on v5

--- a/solution.py
+++ b/solution.py
@@ -175,22 +175,20 @@
 
     my_chunk = me // SLABS
 
-    def send_bins(step, carry):
-        there = lax.rem(me + step, SEGS)
+    def send_bins(step, to_side):
+        there_work = lax.rem(work + step, WORKS)
         pltpu.make_async_remote_copy(
-            src_ref=send_in.at[
-                slot_of((there // 4) * 2 + lax.rem(there, 2), lax.rem(there // 2, 2))
-            ],
+            src_ref=send_in.at[slot_of(there_work, to_side)],
             dst_ref=recv_in.at[me],
             send_sem=in_send_sem,
             recv_sem=in_recv_sem.at[my_chunk],
-            device_id=to_seg(there),
+            device_id=to_seg(device_of(there_work, to_side)),
             device_id_type=MESH,
         ).start()
-        return carry
-
-    lax.fori_loop(1, SEGS, send_bins, 0)
-    pltpu.make_async_copy(send_in.at[my_slot], recv_in.at[me], in_recv_sem.at[my_chunk]).start()
+        return to_side
+
+    lax.fori_loop(0, WORKS, send_bins, 1 - side)
+
 
     def hold(to_side):
         return tgt_raw.at[pl.ds(2 * to_side, 2)], tgt.at[pl.ds(2 * core, 2)]
@@ -205,6 +203,8 @@
         device_id_type=MESH,
     )
     tgt_across.start()
+    lax.fori_loop(1, WORKS, send_bins, side)
+    pltpu.make_async_copy(send_in.at[my_slot], recv_in.at[me], in_recv_sem.at[my_chunk]).start()
     near_source, near_place = hold(side)
     near_stays = core == side
 
@@ -512,7 +512,8 @@
             for i, block in enumerate(swap_lane_groups(by_clip)):
                 send_out[tile * 8 + g * 4 + i] = block.astype(BF16)
         for i in range(8):
-            there = tile * 8 + i
+            to_side = 1 - side if i < 4 else side
+            there = tile * 8 + (i // 2 % 2) * 4 + to_side * 2 + i % 2
 
             @pl.when(there != me)
             def _():

time: 62.7 us -> 62.8 us (level)
  no operation moved by 1% of the time
where the time goes in v6:
time: 62.8 us; the launch traced here: 62.2 us
  Pallas kernels  58 us (92%)
  between operations  2.39 us (4%)
  local copies, waits for them, and re-layouts  1.77 us (3%)
    pallas_call x1, Pallas kernels, body(): pl.pallas_call(kernel, out_shape=(jax.ShapeDtypeStruct((ROWS, FRAMES), BF...  58 us
    unnamed x1, local copies, waits for them, and re-layouts  1.77 us

profile of v6, /device:TPU:33, one launch (start us, length us, event | category | flops | bytes accessed | tf_op | source)
XLA Modules:
  0.0 62.2 jit_solution(9990876450922590251)
XLA Ops:
  0.6 58.0 %shard_map.86 = (bf16[128,1536]{1,0:T(8,128)(2,1)}, f32[1,128]{1,0:T(1,128)}) custom-call(bf16[128,1536]{1,0:T(8,128)(2,1)} %bitcast.5, bf16[4,12288]{1,0:T(4,128)(2,1)} %target_ref.1, s32[4]{0:T(128)} %lengths_ref.1, bf16[2048,2048]{1,0:T(8,128)(2,1)} %constant.8.clone.syn_hbm, bf16[512,512]{1,0:T(8,128)(2,1)} %constant.9.clone.a512_hbm, ...), custom_call_target="tpu_custom_call" | custom-call | flops 8000000000 | bytes 20000000 | tf_op jit(solution)/shard_map/pallas_call | solution.py:601
  59.3 1.8 %copy.12 = bf16[4,2,16,1536]{3,2,1,0:T(8,128)(2,1)} copy(bf16[4,2,16,1536]{3,2,1,0:T(8,128)(2,1)} %bitcast.4) | data formatting | bytes 786432

commit v7 on v5

--- a/solution.py
+++ b/solution.py
@@ -362,7 +362,7 @@
             return energy
 
         start = jnp.zeros((LOCAL_CLIPS, 8, 128), F32)
-        sums[3 + level] = lax.fori_loop(0, half // 256, target_columns, start)
+        sums[3 + level] = lax.fori_loop(0, half // 256, target_columns, start, unroll=True)
 
     for copy in est_copies:
         copy.wait_recv()

time: 62.7 us -> 62.2 us (level)
  no operation moved by 1% of the time
where the time goes in v7:
time: 62.2 us; the launch traced here: 61.6 us
  Pallas kernels  57.5 us (92%)
  between operations  2.39 us (4%)
  local copies, waits for them, and re-layouts  1.77 us (3%)
    pallas_call x1, Pallas kernels, body(): pl.pallas_call(kernel, out_shape=(jax.ShapeDtypeStruct((ROWS, FRAMES), BF...  57.5 us
    unnamed x1, local copies, waits for them, and re-layouts  1.77 us

profile of v7, /device:TPU:33, one launch (start us, length us, event | category | flops | bytes accessed | tf_op | source)
XLA Modules:
  0.0 61.6 jit_solution(7404790314428730422)
XLA Ops:
  0.6 57.5 %shard_map.86 = (bf16[128,1536]{1,0:T(8,128)(2,1)}, f32[1,128]{1,0:T(1,128)}) custom-call(bf16[128,1536]{1,0:T(8,128)(2,1)} %bitcast.5, bf16[4,12288]{1,0:T(4,128)(2,1)} %target_ref.1, s32[4]{0:T(128)} %lengths_ref.1, bf16[2048,2048]{1,0:T(8,128)(2,1)} %constant.8.clone.syn_hbm, bf16[512,512]{1,0:T(8,128)(2,1)} %constant.9.clone.a512_hbm, ...), custom_call_target="tpu_custom_call" | custom-call | flops 8000000000 | bytes 20000000 | tf_op jit(solution)/shard_map/pallas_call | solution.py:600
  58.7 1.8 %copy.12 = bf16[4,2,16,1536]{3,2,1,0:T(8,128)(2,1)} copy(bf16[4,2,16,1536]{3,2,1,0:T(8,128)(2,1)} %bitcast.4) | data formatting | bytes 786432
